TPU v7x, 1024 devices: a whole 4x4x32 slice. The times are simulated.
1024 devices in a mesh: dp: 128 (over x, y, z_hi, core), expert: 8 (over z_lo).
Axes of the slice: x: 4, y: 4, z: 32 (z_hi: 4, z_lo: 8; z = z_hi * 8 + z_lo), core: 2. Of those that a mesh axis runs over, the one named last changes fastest.
Arguments:
- d_out: bfloat16 [131072, 2048], P(('dp', 'expert')), may hold values from -0.09375 to 0.09375
- router_weight: float32 [131072, 2], P(('dp', 'expert')), may hold values from 0.05 to 0.95
- routes: int32 [131072, 2], P(('dp', 'expert')), may hold values from 0 to 15, all different within a row; in each aligned block of 128 rows (0 to 127, 128 to 255, ...) at most 32 rows name the same one
- gate_pre: bfloat16 [32768, 7168], P('dp'), may hold values from -6 to 6
- up_pre: bfloat16 [32768, 7168], P('dp'), may hold values from -24 to 24
Outputs:
- grad_down: float32 [7168, 2048], P('dp', 'expert')
Inputs may be any that keep to these rules, and one draw needn't show every extreme that they name: `routes`: each row names two different experts. In each aligned block of 128 rows (one device's tokens) no expert is named by more than 32 rows, a bound that some block reaches.
All inputs are finite; a program needn't handle non-finite values.
Results may differ from a plain program's by a relative error of at most 0.004.
Values may be sent and summed in bfloat16 or wider, within the bound.
No kernel may reach another device: no remote copies, remote signals or barrier semaphores. Data moves between devices by JAX's collectives and lax.ppermute only.
A program may use at most 64 MiB of HBM per device.

v0:
```python
import jax
import jax.numpy as jnp
from jax import lax
from jax.sharding import PartitionSpec as P


def term_maker(hidden, columns):
    return lax.dot_general(
        hidden, columns, (((0,), (0,)), ((), ())), preferred_element_type=jnp.float32
    )


def body(d_out, router_weight, routes, gate_pre, up_pre):
    tokens_here = d_out.shape[0]
    feature_count = d_out.shape[1]
    expert_count = lax.axis_size("expert")
    slot_count = gate_pre.shape[0]
    capacity = slot_count // expert_count
    marked = (routes.reshape(-1) == 0).astype(jnp.int32)
    position = jnp.cumsum(marked, dtype=jnp.int32) - marked
    target = jnp.where(marked == 1, position, capacity)
    scaled = (d_out.astype(jnp.float32)[:, None, :] * router_weight[:, :, None]).astype(
        jnp.bfloat16
    )
    scaled = scaled.reshape(2 * tokens_here, feature_count)
    outgoing = (
        jnp.zeros((capacity, feature_count), jnp.bfloat16).at[target].set(scaled, mode="drop")
    )
    incoming = lax.all_to_all(outgoing, "expert", split_axis=1, concat_axis=0, tiled=True)
    hidden = (jax.nn.silu(gate_pre.astype(jnp.float32)) * up_pre.astype(jnp.float32)).astype(
        jnp.bfloat16
    )
    result = lax.psum_scatter(term_maker(hidden, incoming), "dp", scatter_dimension=0, tiled=True)
    return result


def solution(mesh):
    placed = (
        P(("dp", "expert"), None),
        P(("dp", "expert"), None),
        P(("dp", "expert"), None),
        P("dp", None),
        P("dp", None),
    )
    return jax.shard_map(
        body, mesh=mesh, in_specs=placed, out_specs=P("dp", "expert"), check_vma=False
    )
```

profile of v0, /device:TPU:1, one launch (start us, length us, event | category | flops | bytes accessed | tf_op | source)
XLA Modules:
  0.0 1201.7 jit_solution(6364069367278121024)
XLA Ops:
  6.5 0.0 reduce-scatter.2.cloned.1.call-start
  6.5 0.7 compare_convert_fusion
  7.2 0.1 copy.13
  7.3 0.1 reshape.82
  7.5 0.1 reshape.81
  7.6 0.3 reduce-window.9
  7.9 0.1 slice.7
  8.0 0.1 slice_reduce_fusion
  8.2 0.1 broadcast_add_fusion
  8.2 0.8 copy.15
  9.0 0.1 mul.29
  9.2 2.1 mul.27
  11.3 2.5 mul.28
  13.8 3.1 scatter_custom_fusion
  16.9 23.1 %all_to_all.19 = bf16[32,8,256]{2,0,1:T(8,128)(2,1)S(1)} all-to-all(bf16[32,8,256]{2,0,1:T(8,128)(2,1)S(1)} %bitcast.12), channel_id=1, replica_groups=mesh['dp'=128,'expert'=8] {'expert'}, dimensions={1} | all-to-all | bytes 262144 | tf_op jit(solution)/shard_map/all_to_all | solution.py:29
  40.1 9.0 fusion.5
  49.1 0.0 reduce-scatter.2.cloned.1.call-update
  49.1 1145.7 %reduce-scatter.2.cloned.1.call-done = f32[56,256]{1,0:T(8,128)} async-done(((f32[7168,256]{1,0:T(8,128)}), f32[56,256]{1,0:T(8,128)}) %reduce-scatter.2.cloned.1.call-update) | async-done | bytes 57360 | tf_op jit(solution)/shard_map/reduce_scatter | solution.py:33
  (3 shorter events, 0.1 us)
Async XLA Ops:
  6.5 1188.3 %reduce-scatter.2.cloned.1.call-start = ((), (), s32[]{:S(2)}) async-start(), calls=%async_computation.2 | async-start | bytes 7397376 | tf_op jit(solution)/shard_map/reduce_scatter | solution.py:33
Sparse Core Ops, SparseCore 0:
  49.2 1145.5 reduce-scatter.1
where the time goes:
time: 1210 us; the launch traced here: 1200 us
  waiting for transfers between devices  1150 us (95%)
  blocking collectives  23.1 us (2%)
  between operations  13.4 us (1%)
    reduce_scatter x1, waiting for transfers between devices, body(): lax.psum_scatter(term_maker(hidden, incoming), 'dp', scatter_dimension=0,...  1150 us
  transfers between devices with their start and end apart: 1, of which 1 were waited for; matrix products, arithmetic and copies ran while one was open for 0% of the time, Pallas kernels for 0%

commit v1 on v0

v1 whole, which is shorter than its diff:
```python
import jax
import jax.numpy as jnp
from jax import lax
from jax.sharding import Mesh, PartitionSpec as P

GRID = (("x", 4), ("y", 4), ("far", 4), ("core", 2))
SWAP = [(0, 1), (1, 0)]


def body(d_out, router_weight, routes, gate_pre, up_pre):
    group_count = lax.axis_size("expert")
    capacity = gate_pre.shape[0] // group_count
    planes = lax.axis_size("x") * lax.axis_size("y")
    fars = lax.axis_size("far")
    rows, units = gate_pre.shape
    width = d_out.shape[1] // group_count
    block = units // (planes * fars * 2)
    core = lax.axis_index("core")
    far = lax.axis_index("far")

    hidden = (jax.nn.silu(gate_pre.astype(jnp.float32)) * up_pre.astype(jnp.float32)).astype(
        jnp.bfloat16
    )
    turned = hidden.T.reshape(planes * fars, 2, block, rows)
    mine = lax.dynamic_index_in_dim(turned, core, 1, False).reshape(-1, rows)
    theirs = lax.dynamic_index_in_dim(turned, 1 - core, 1, False).reshape(-1, rows)
    met = lax.ppermute(theirs, "core", SWAP)

    named = routes == 0
    marked = jnp.any(named, axis=1)
    weight = jnp.sum(jnp.where(named, router_weight, 0.0), axis=1)
    count = marked.astype(jnp.int32)
    position = jnp.cumsum(count, dtype=jnp.int32) - count
    slots = lax.broadcasted_iota(jnp.int32, (capacity, d_out.shape[0]), 0)
    chosen = ((slots == position[None, :]) & marked[None, :]).astype(jnp.bfloat16)
    scaled = (d_out.astype(jnp.float32) * weight[:, None]).astype(jnp.bfloat16)
    outgoing = jnp.dot(chosen, scaled, preferred_element_type=jnp.float32).astype(jnp.bfloat16)
    incoming = lax.all_to_all(outgoing, "expert", split_axis=1, concat_axis=0, tiled=True)
    incoming_met = lax.ppermute(incoming, "core", SWAP)

    partial = jnp.dot(mine, incoming, preferred_element_type=jnp.float32) + jnp.dot(
        met, incoming_met, preferred_element_type=jnp.float32
    )
    partial = partial.astype(jnp.bfloat16).reshape(planes, fars * block, width)
    partial = lax.all_to_all(partial, ("x", "y"), split_axis=0, concat_axis=0, tiled=True)
    partial = jnp.sum(partial.astype(jnp.float32), axis=0).reshape(fars, block, width)
    result = lax.dynamic_index_in_dim(partial, far, 0, False)
    for step in range(1, fars):
        piece = lax.dynamic_index_in_dim(partial, (far + step) % fars, 0, False)
        piece = piece.astype(jnp.bfloat16)
        piece = lax.ppermute(piece, "far", [(i, (i + step) % fars) for i in range(fars)])
        result = result + piece.astype(jnp.float32)
    return result


def solution(mesh):
    names = tuple(name for name, _ in GRID)
    sizes = tuple(size for _, size in GRID)
    fine = Mesh(mesh.devices.reshape(sizes + (mesh.shape["expert"],)), names + ("expert",))
    tokens = P(names + ("expert",), None)
    slots = P(names, None)
    return jax.shard_map(
        body,
        mesh=fine,
        in_specs=(tokens, tokens, tokens, slots, slots),
        out_specs=P(names, "expert"),
        check_vma=False,
    )
```

time: 1210 us -> 134 us (0.11)
  waiting for transfers between devices: 1150 us -> 33.8 us
  starting transfers between devices: 0.01 us -> 58.8 us
  between operations: 13.4 us -> 0.17 us
    reduce_scatter x1 -> x0, waiting for transfers between devices: 1150 us -> none  [body(): lax.psum_scatter(term_maker(hidden, incoming), 'dp', scatter_dimension=0,...]
    ppermute x0 -> x5, starting transfers between devices: none -> 55.1 us  [the longest x3 35.2 us: body(): lax.ppermute(piece, 'far', [(i, (i + step) % fars) for i in range(fars)])]
    all_to_all x0 -> x1, waiting for transfers between devices: none -> 25.8 us  [body(): lax.all_to_all(partial, ('x', 'y'), split_axis=0, concat_axis=0, tiled=True)]
  transfers between devices with their start and end apart: 1 -> 6, of which waited for: 1 -> 4; matrix products, arithmetic and copies ran while one was open for 0% -> 1% of each run, Pallas kernels for 0% -> 0%
where the time goes in v1:
time: 134 us; the launch traced here: 133 us
  starting transfers between devices  58.8 us (44%)
  waiting for transfers between devices  33.8 us (25%)
  local copies, waits for them, and re-layouts  15.6 us (12%)
  blocking collectives  13.3 us (10%)
  other arithmetic  6.83 us (5%)
  matrix products  4.33 us (3%)
    ppermute x3, starting transfers between devices, body(): lax.ppermute(piece, 'far', [(i, (i + step) % fars) for i in range(fars)])  35.2 us
    all_to_all x1, waiting for transfers between devices, body(): lax.all_to_all(partial, ('x', 'y'), split_axis=0, concat_axis=0, tiled=True)  25.8 us
    ppermute x1, starting transfers between devices, body(): met = lax.ppermute(theirs, 'core', SWAP)  16.1 us
    all_to_all x1, blocking collectives, body(): lax.all_to_all(outgoing, 'expert', split_axis=1, concat_axis=0, tiled=True)  13.3 us
    unnamed x8, local copies, waits for them, and re-layouts  11.8 us
    ppermute x3, waiting for transfers between devices, body(): lax.ppermute(piece, 'far', [(i, (i + step) % fars) for i in range(fars)])  7.65 us
    convert_element_type x1, other arithmetic, body(): (jax.nn.silu(gate_pre.astype(jnp.float32)) * up_pre.astype(jnp.float32))....  5.61 us
    ppermute x1, starting transfers between devices, body(): incoming_met = lax.ppermute(incoming, 'core', SWAP)  3.84 us
  transfers between devices with their start and end apart: 6, of which 4 were waited for; matrix products, arithmetic and copies ran while one was open for 1% of the time, Pallas kernels for 0%

profile of v1, /device:TPU:1, one launch (start us, length us, event | category | flops | bytes accessed | tf_op | source)
XLA Modules:
  0.0 132.9 jit_solution(11615035893330613922)
XLA Ops:
  0.0 5.9 %copy.8 = bf16[256,7168]{0,1:T(8,128)(2,1)} copy(bf16[256,7168]{1,0:T(8,128)(2,1)} %param.9) | data formatting | bytes 7340032 | tf_op args[4]
  5.9 5.9 %copy.7 = bf16[256,7168]{0,1:T(8,128)(2,1)} copy(bf16[256,7168]{1,0:T(8,128)(2,1)} %param.8) | data formatting | bytes 7340032 | tf_op args[3]
  11.8 5.6 %fusion.4 = bf16[256,7168]{0,1:T(8,128)(2,1)} fusion(bf16[256,7168]{0,1:T(8,128)(2,1)} %copy.8, bf16[256,7168]{0,1:T(8,128)(2,1)} %copy.7), kind=kLoop, calls=%fused_computation.6 | loop fusion | flops 14680064 | bytes 11010048 | tf_op jit(solution)/shard_map/convert_element_type | solution.py:21
  17.5 0.0 copy-start.2
  17.5 0.0 copy-start.1
  17.5 0.0 copy-start
  17.5 3.6 %constant_dynamic-slice_fusion = (bf16[64,1,56,256]{3,2,1,0:T(8,128)(2,1)}, bf16[64,1,56,256]{3,2,1,0:T(8,128)(2,1)S(1)}) fusion(bf16[64,2,56,256]{3,2,1,0:T(8,128)(2,1)} %bitcast.32, s32[]{:T(128)S(6)} %select_n.41, s32[]{:T(128)S(6)} %select_n.39), kind=kLoop, calls=%fused_computation.27 | loop fusion | bytes 7340040 | tf_op jit(solution)/shard_map/jit(dynamic_index_in_dim)/dynamic_slice | solution.py:26
  21.1 16.1 %collective-permute-start = (bf16[3584,256]{1,0:T(8,128)(2,1)}, bf16[3584,256]{1,0:T(8,128)(2,1)}, u32[]{:S(2)}, u32[]{:S(2)}) collective-permute-start(bf16[3584,256]{1,0:T(8,128)(2,1)} %bitcast.7), channel_id=1, source_target_pairs={{0,8},{8,0},{1,9},{9,1},{2,10},{10,2},{3,11},{11,3},{4,12},{12,4},... | collective-permute-start | bytes 5505032 | tf_op jit(solution)/shard_map/ppermute | solution.py:27
  37.1 0.0 copy-done.2
  37.2 0.1 copy.9
  37.3 0.2 reduce-window.8
  37.5 0.1 reduce
  37.6 0.0 copy-done.1
  37.6 0.0 copy-done
  37.6 0.3 convolution_convert_fusion
  37.9 13.3 %all_to_all.24 = bf16[32,8,256]{2,0,1:T(8,128)(2,1)S(1)} all-to-all(bf16[32,8,256]{2,0,1:T(8,128)(2,1)S(1)} %bitcast.38), channel_id=1, replica_groups=mesh['x'=4,'y'=4,'far'=4,'core'=2,'expert'=8] {'expert'}, dimensions={1} | all-to-all | bytes 262144 | tf_op jit(solution)/shard_map/all_to_all | solution.py:38
  51.3 3.8 %collective-permute-start.1 = (bf16[256,256]{1,0:T(8,128)(2,1)S(1)}, bf16[256,256]{1,0:T(8,128)(2,1)S(1)}, u32[]{:S(2)}, u32[]{:S(2)}) collective-permute-start(bf16[256,256]{1,0:T(8,128)(2,1)S(1)} %bitcast.36), channel_id=1, source_target_pairs={{0,8},{8,0},{1,9},{9,1},{2,10},{10,2},{3,11},{11,3},{4,12},{12,4},... | collective-permute-start | bytes 393224 | tf_op jit(solution)/shard_map/ppermute | solution.py:39
  55.1 0.6 fusion.17
  55.7 0.3 collective-permute-done.1
  56.1 0.0 collective-permute-done
  56.1 3.4 %fusion.5 = bf16[3584,256]{1,0:T(8,128)(2,1)} fusion(f32[3584,256]{1,0:T(8,128)S(1)} %fusion.17, bf16[3584,256]{1,0:T(8,128)(2,1)} %collective-permute-done, bf16[256,256]{1,0:T(8,128)(2,1)S(1)} %collective-permute-done.1), kind=kOutput, calls=%fused_computation.8 | convolution fusion | flops 471597056 | bytes 7471104 | tf_op jit(solution)/shard_map/dot_general | solution.py:41
  59.5 3.7 %all-to-all-start.1 = ((bf16[16,224,256]{2,1,0:T(8,128)(2,1)}), bf16[16,224,256]{2,1,0:T(8,128)(2,1)S(1)}, u32[]{:S(2)}, u32[]{:S(2)}) async-start(bf16[16,224,256]{2,1,0:T(8,128)(2,1)} %bitcast.9), calls=%async_computation.1 | async-start | bytes 3670016 | tf_op jit(solution)/shard_map/all_to_all | solution.py:45
  63.3 25.8 %all-to-all-done.1 = bf16[16,224,256]{2,1,0:T(8,128)(2,1)S(1)} async-done(((bf16[16,224,256]{2,1,0:T(8,128)(2,1)}), bf16[16,224,256]{2,1,0:T(8,128)(2,1)S(1)}, u32[]{:S(2)}, u32[]{:S(2)}) %all-to-all-start.1) | async-done | bytes 1835040 | tf_op jit(solution)/shard_map/all_to_all | solution.py:45
  89.1 0.2 convert_reduce_fusion
  89.4 15.2 %collective-permute-start.4 = (bf16[56,256]{1,0:T(8,128)(2,1)S(1)}, bf16[56,256]{1,0:T(8,128)(2,1)S(1)}, u32[]{:S(2)}, u32[]{:S(2)}) collective-permute-start(bf16[56,256]{1,0:T(8,128)(2,1)S(1)} %get-tuple-element.8), channel_id=1, source_target_pairs={{0,48},{16,0},{32,16},{48,32},{1,49},{17,1},{33,17},{49,33},{2,50}... | collective-permute-start | bytes 86024 | tf_op jit(solution)/shard_map/ppermute | solution.py:51
  104.6 12.0 %collective-permute-start.3 = (bf16[56,256]{1,0:T(8,128)(2,1)S(1)}, bf16[56,256]{1,0:T(8,128)(2,1)S(1)}, u32[]{:S(2)}, u32[]{:S(2)}) collective-permute-start(bf16[56,256]{1,0:T(8,128)(2,1)S(1)} %get-tuple-element.9), channel_id=1, source_target_pairs={{0,32},{16,48},{32,0},{48,16},{1,33},{17,49},{33,1},{49,17},{2,34}... | collective-permute-start | bytes 86024 | tf_op jit(solution)/shard_map/ppermute | solution.py:51
  116.7 7.9 %collective-permute-start.2 = (bf16[56,256]{1,0:T(8,128)(2,1)S(1)}, bf16[56,256]{1,0:T(8,128)(2,1)S(1)}, u32[]{:S(2)}, u32[]{:S(2)}) collective-permute-start(bf16[56,256]{1,0:T(8,128)(2,1)S(1)} %get-tuple-element.7), channel_id=1, source_target_pairs={{0,16},{16,32},{32,48},{48,0},{1,17},{17,33},{33,49},{49,1},{2,18}... | collective-permute-start | bytes 86024 | tf_op jit(solution)/shard_map/ppermute | solution.py:51
  124.6 0.0 collective-permute-done.4
  124.6 3.2 %collective-permute-done.3 = bf16[56,256]{1,0:T(8,128)(2,1)S(1)} collective-permute-done((bf16[56,256]{1,0:T(8,128)(2,1)S(1)}, bf16[56,256]{1,0:T(8,128)(2,1)S(1)}, u32[]{:S(2)}, u32[]{:S(2)}) %collective-permute-start.3) | collective-permute-done | bytes 28704 | tf_op jit(solution)/shard_map/ppermute | solution.py:51
  127.8 4.5 %collective-permute-done.2 = bf16[56,256]{1,0:T(8,128)(2,1)S(1)} collective-permute-done((bf16[56,256]{1,0:T(8,128)(2,1)S(1)}, bf16[56,256]{1,0:T(8,128)(2,1)S(1)}, u32[]{:S(2)}, u32[]{:S(2)}) %collective-permute-start.2) | collective-permute-done | bytes 28704 | tf_op jit(solution)/shard_map/ppermute | solution.py:51
  132.3 0.6 fusion.8
  (6 shorter events, 0.1 us)
Async XLA Ops:
  17.5 19.7 %copy-start.2 = (s32[128,2]{0,1:T(2,128)S(1)}, s32[128,2]{0,1:T(2,128)}, u32[]{:S(2)}) copy-start(s32[128,2]{0,1:T(2,128)} %param.7) | copy-start | bytes 3076
  17.5 20.1 %copy-start.1 = (f32[128,2]{0,1:T(2,128)S(1)}, f32[128,2]{0,1:T(2,128)}, u32[]{:S(2)}) copy-start(f32[128,2]{0,1:T(2,128)} %param.6) | copy-start | bytes 3076
  17.5 20.2 %copy-start = (bf16[128,2048]{1,0:T(8,128)(2,1)S(1)}, bf16[128,2048]{1,0:T(8,128)(2,1)}, u32[]{:S(2)}) copy-start(bf16[128,2048]{1,0:T(8,128)(2,1)} %param.5) | copy-start | bytes 1572868
  21.1 35.0 %collective-permute-start = (bf16[3584,256]{1,0:T(8,128)(2,1)}, bf16[3584,256]{1,0:T(8,128)(2,1)}, u32[]{:S(2)}, u32[]{:S(2)}) collective-permute-start(bf16[3584,256]{1,0:T(8,128)(2,1)} %bitcast.7), channel_id=1, source_target_pairs={{0,8},{8,0},{1,9},{9,1},{2,10},{10,2},{3,11},{11,3},{4,12},{12,4},... | collective-permute-start | bytes 5505032 | tf_op jit(solution)/shard_map/ppermute | solution.py:27
  51.3 4.8 %collective-permute-start.1 = (bf16[256,256]{1,0:T(8,128)(2,1)S(1)}, bf16[256,256]{1,0:T(8,128)(2,1)S(1)}, u32[]{:S(2)}, u32[]{:S(2)}) collective-permute-start(bf16[256,256]{1,0:T(8,128)(2,1)S(1)} %bitcast.36), channel_id=1, source_target_pairs={{0,8},{8,0},{1,9},{9,1},{2,10},{10,2},{3,11},{11,3},{4,12},{12,4},... | collective-permute-start | bytes 393224 | tf_op jit(solution)/shard_map/ppermute | solution.py:39
  59.5 29.6 %all-to-all-start.1 = ((bf16[16,224,256]{2,1,0:T(8,128)(2,1)}), bf16[16,224,256]{2,1,0:T(8,128)(2,1)S(1)}, u32[]{:S(2)}, u32[]{:S(2)}) async-start(bf16[16,224,256]{2,1,0:T(8,128)(2,1)} %bitcast.9), calls=%async_computation.1 | async-start | bytes 3670016 | tf_op jit(solution)/shard_map/all_to_all | solution.py:45
  89.4 35.2 %collective-permute-start.4 = (bf16[56,256]{1,0:T(8,128)(2,1)S(1)}, bf16[56,256]{1,0:T(8,128)(2,1)S(1)}, u32[]{:S(2)}, u32[]{:S(2)}) collective-permute-start(bf16[56,256]{1,0:T(8,128)(2,1)S(1)} %get-tuple-element.8), channel_id=1, source_target_pairs={{0,48},{16,0},{32,16},{48,32},{1,49},{17,1},{33,17},{49,33},{2,50}... | collective-permute-start | bytes 86024 | tf_op jit(solution)/shard_map/ppermute | solution.py:51
  104.6 23.2 %collective-permute-start.3 = (bf16[56,256]{1,0:T(8,128)(2,1)S(1)}, bf16[56,256]{1,0:T(8,128)(2,1)S(1)}, u32[]{:S(2)}, u32[]{:S(2)}) collective-permute-start(bf16[56,256]{1,0:T(8,128)(2,1)S(1)} %get-tuple-element.9), channel_id=1, source_target_pairs={{0,32},{16,48},{32,0},{48,16},{1,33},{17,49},{33,1},{49,17},{2,34}... | collective-permute-start | bytes 86024 | tf_op jit(solution)/shard_map/ppermute | solution.py:51
  116.7 15.6 %collective-permute-start.2 = (bf16[56,256]{1,0:T(8,128)(2,1)S(1)}, bf16[56,256]{1,0:T(8,128)(2,1)S(1)}, u32[]{:S(2)}, u32[]{:S(2)}) collective-permute-start(bf16[56,256]{1,0:T(8,128)(2,1)S(1)} %get-tuple-element.7), channel_id=1, source_target_pairs={{0,16},{16,32},{32,48},{48,0},{1,17},{17,33},{33,49},{49,1},{2,18}... | collective-permute-start | bytes 86024 | tf_op jit(solution)/shard_map/ppermute | solution.py:51

commit v2 on v1

--- a/solution.py
+++ b/solution.py
@@ -1,10 +1,91 @@
+import functools
+
 import jax
 import jax.numpy as jnp
 from jax import lax
+from jax.experimental import pallas as pl
+from jax.experimental.pallas import tpu as pltpu
 from jax.sharding import Mesh, PartitionSpec as P
 
 GRID = (("x", 4), ("y", 4), ("far", 4), ("core", 2))
 SWAP = [(0, 1), (1, 0)]
+PARTS = 8
+
+
+def hidden_kernel(block, core_ref, gate_ref, up_ref, mine_ref, theirs_ref, gate, up, sems):
+    parts, rows, part = gate.shape
+
+    def copies(index):
+        columns = pl.ds(index * part, part)
+        return (
+            pltpu.make_async_copy(gate_ref.at[:, columns], gate.at[index], sems.at[0, index]),
+            pltpu.make_async_copy(up_ref.at[:, columns], up.at[index], sems.at[1, index]),
+        )
+
+    for index in range(parts):
+        for copy in copies(index):
+            copy.start()
+    core = core_ref[0]
+    for index in range(parts):
+        for copy in copies(index):
+            copy.wait()
+        value = gate[index].astype(jnp.float32)
+        value = value * (0.5 * jnp.tanh(0.5 * value) + 0.5) * up[index].astype(jnp.float32)
+        value = value.astype(jnp.bfloat16).astype(jnp.float32)
+        value = value.T.reshape(part // (2 * block), 2, block, rows)
+        first = value[:, 0].reshape(part // 2, rows).astype(jnp.bfloat16)
+        second = value[:, 1].reshape(part // 2, rows).astype(jnp.bfloat16)
+        where = slice(index * (part // 2), (index + 1) * (part // 2))
+
+        @pl.when(core == 0)
+        def _():
+            mine_ref[where, :] = first
+            theirs_ref[where, :] = second
+
+        @pl.when(core != 0)
+        def _():
+            mine_ref[where, :] = second
+            theirs_ref[where, :] = first
+
+
+def hidden_halves(core, gate_pre, up_pre, block):
+    rows, units = gate_pre.shape
+    half = jax.ShapeDtypeStruct((units // 2, rows), jnp.bfloat16)
+    buffer = pltpu.VMEM((PARTS, rows, units // PARTS), jnp.bfloat16)
+    return pl.pallas_call(
+        functools.partial(hidden_kernel, block),
+        in_specs=[
+            pl.BlockSpec(memory_space=pltpu.SMEM),
+            pl.BlockSpec(memory_space=pl.ANY),
+            pl.BlockSpec(memory_space=pl.ANY),
+        ],
+        out_specs=[pl.BlockSpec(memory_space=pltpu.VMEM)] * 2,
+        out_shape=[half, half],
+        scratch_shapes=[buffer, buffer, pltpu.SemaphoreType.DMA((2, PARTS))],
+        compiler_params=pltpu.CompilerParams(vmem_limit_bytes=52 << 20),
+        cost_estimate=pl.CostEstimate(
+            flops=8 * rows * units, bytes_accessed=6 * rows * units, transcendentals=rows * units
+        ),
+        name="hidden",
+    )(core.reshape(1), gate_pre, up_pre)
+
+
+def sum_kernel(terms_ref, sum_ref):
+    total = terms_ref[0].astype(jnp.float32)
+    for index in range(1, terms_ref.shape[0]):
+        total = total + terms_ref[index].astype(jnp.float32)
+    sum_ref[...] = total.astype(jnp.bfloat16)
+
+
+def summed(terms):
+    return pl.pallas_call(
+        sum_kernel,
+        in_specs=[pl.BlockSpec(memory_space=pltpu.VMEM)],
+        out_specs=pl.BlockSpec(memory_space=pltpu.VMEM),
+        out_shape=jax.ShapeDtypeStruct(terms.shape[1:], jnp.bfloat16),
+        compiler_params=pltpu.CompilerParams(vmem_limit_bytes=16 << 20),
+        name="plane_sum",
+    )(terms)
 
 
 def body(d_out, router_weight, routes, gate_pre, up_pre):
@@ -16,14 +97,8 @@
     width = d_out.shape[1] // group_count
     block = units // (planes * fars * 2)
     core = lax.axis_index("core")
-    far = lax.axis_index("far")
 
-    hidden = (jax.nn.silu(gate_pre.astype(jnp.float32)) * up_pre.astype(jnp.float32)).astype(
-        jnp.bfloat16
-    )
-    turned = hidden.T.reshape(planes * fars, 2, block, rows)
-    mine = lax.dynamic_index_in_dim(turned, core, 1, False).reshape(-1, rows)
-    theirs = lax.dynamic_index_in_dim(turned, 1 - core, 1, False).reshape(-1, rows)
+    mine, theirs = hidden_halves(core, gate_pre, up_pre, block)
     met = lax.ppermute(theirs, "core", SWAP)
 
     named = routes == 0
@@ -43,14 +118,9 @@
     )
     partial = partial.astype(jnp.bfloat16).reshape(planes, fars * block, width)
     partial = lax.all_to_all(partial, ("x", "y"), split_axis=0, concat_axis=0, tiled=True)
-    partial = jnp.sum(partial.astype(jnp.float32), axis=0).reshape(fars, block, width)
-    result = lax.dynamic_index_in_dim(partial, far, 0, False)
-    for step in range(1, fars):
-        piece = lax.dynamic_index_in_dim(partial, (far + step) % fars, 0, False)
-        piece = piece.astype(jnp.bfloat16)
-        piece = lax.ppermute(piece, "far", [(i, (i + step) % fars) for i in range(fars)])
-        result = result + piece.astype(jnp.float32)
-    return result
+    partial = summed(partial).reshape(fars, block, width)
+    partial = lax.all_to_all(partial, "far", split_axis=0, concat_axis=0, tiled=True)
+    return jnp.sum(partial.astype(jnp.float32), axis=0)
 
 
 def solution(mesh):

time: 134 us -> 119 us (0.89)
  the two profiles are of different devices: /device:TPU:1 before, /device:TPU:34 now
where the time goes in v2:
time: 119 us; the launch traced here: 118 us
  blocking collectives  104 us (87%)
  Pallas kernels  6.02 us (5%)
  starting transfers between devices  3.83 us (3%)
  matrix products  3.08 us (3%)
    all_to_all x1, blocking collectives, body(): lax.all_to_all(partial, 'far', split_axis=0, concat_axis=0, tiled=True)  48.4 us
    all_to_all x1, blocking collectives, body(): lax.all_to_all(partial, ('x', 'y'), split_axis=0, concat_axis=0, tiled=True)  31.2 us
    all_to_all x1, blocking collectives, body(): lax.all_to_all(outgoing, 'expert', split_axis=1, concat_axis=0, tiled=True)  24.1 us
    pallas_call x1, Pallas kernels, hidden_halves(): pl.pallas_call(functools.partial(hidden_kernel, block), in_specs=[pl.Bloc...  5.78 us
  transfers between devices with their start and end apart: 2, of which 1 were waited for; matrix products, arithmetic and copies ran while one was open for 1% of the time, Pallas kernels for 0%

profile of v2, /device:TPU:34, one launch (start us, length us, event | category | flops | bytes accessed | tf_op | source)
XLA Modules:
  0.0 118.5 jit_solution(15682493526218270512)
XLA Ops:
  0.0 0.0 copy-start.2
  0.0 0.0 copy-start.1
  0.0 0.0 copy-start
  0.0 5.8 %hidden.1 = (bf16[3584,256]{1,0:T(8,128)(2,1)S(1)}, bf16[3584,256]{1,0:T(8,128)(2,1)}) custom-call(s32[1]{0:T(128)} %bitcast.core_ref, bf16[256,7168]{1,0:T(8,128)(2,1)} %gate_ref.1, bf16[256,7168]{1,0:T(8,128)(2,1)} %up_ref.1), custom_call_target="tpu_custom_call" | custom-call | flops 14680064 | bytes 11010048 | tf_op jit(solution)/shard_map/hidden/pallas_call | solution.py:55
  5.8 1.9 %collective-permute-start = (bf16[3584,256]{1,0:T(8,128)(2,1)}, bf16[3584,256]{1,0:T(8,128)(2,1)}, u32[]{:S(2)}, u32[]{:S(2)}) collective-permute-start(bf16[3584,256]{1,0:T(8,128)(2,1)} %get-tuple-element.8), channel_id=1, source_target_pairs={{0,8},{8,0},{1,9},{9,1},{2,10},{10,2},{3,11},{11,3},{4,12},{12,4},... | collective-permute-start | bytes 5505032 | tf_op jit(solution)/shard_map/ppermute | solution.py:102
  7.7 0.0 copy-done.2
  7.8 0.1 copy.7
  7.9 0.2 reduce-window.8
  8.1 0.1 reduce
  8.2 0.0 copy-done.1
  8.2 0.0 copy-done
  8.2 0.3 convolution_convert_fusion
  8.5 24.1 %all_to_all.29 = bf16[32,8,256]{2,0,1:T(8,128)(2,1)S(1)} all-to-all(bf16[32,8,256]{2,0,1:T(8,128)(2,1)S(1)} %bitcast.20), channel_id=1, replica_groups=mesh['x'=4,'y'=4,'far'=4,'core'=2,'expert'=8] {'expert'}, dimensions={1} | all-to-all | bytes 262144 | tf_op jit(solution)/shard_map/all_to_all | solution.py:113
  32.6 1.9 %collective-permute-start.1 = (bf16[256,256]{1,0:T(8,128)(2,1)S(1)}, bf16[256,256]{1,0:T(8,128)(2,1)S(1)}, u32[]{:S(2)}, u32[]{:S(2)}) collective-permute-start(bf16[256,256]{1,0:T(8,128)(2,1)S(1)} %bitcast.18), channel_id=1, source_target_pairs={{0,8},{8,0},{1,9},{9,1},{2,10},{10,2},{3,11},{11,3},{4,12},{12,4},... | collective-permute-start | bytes 393224 | tf_op jit(solution)/shard_map/ppermute | solution.py:114
  34.5 0.6 fusion.7
  35.1 0.7 collective-permute-done.1
  35.8 0.0 collective-permute-done
  35.8 2.2 %fusion = bf16[3584,256]{1,0:T(8,128)(2,1)S(1)} fusion(f32[3584,256]{1,0:T(8,128)S(1)} %fusion.7, bf16[3584,256]{1,0:T(8,128)(2,1)} %collective-permute-done, bf16[256,256]{1,0:T(8,128)(2,1)S(1)} %collective-permute-done.1), kind=kOutput, calls=%fused_computation.1 | convolution fusion | flops 471597056 | bytes 7471104 | tf_op jit(solution)/shard_map/dot_general | solution.py:116
  38.0 31.2 %all_to_all.30.terms_ref = bf16[16,224,256]{2,1,0:T(8,128)(2,1)S(1)} all-to-all(bf16[16,224,256]{2,1,0:T(8,128)(2,1)S(1)} %bitcast.17), channel_id=1, replica_groups=mesh['x'=4,'y'=4,'far'=4,'core'=2,'expert'=8] {'x','y'}, dimensions={0} | all-to-all | bytes 3670016 | tf_op jit(solution)/shard_map/all_to_all | solution.py:120
  69.2 0.2 plane_sum.1
  69.4 48.4 %all_to_all.31 = bf16[4,56,256]{2,1,0:T(8,128)(2,1)S(1)} all-to-all(bf16[4,56,256]{2,1,0:T(8,128)(2,1)S(1)} %bitcast.16), channel_id=1, replica_groups=mesh['x'=4,'y'=4,'far'=4,'core'=2,'expert'=8] {'far'}, dimensions={0} | all-to-all | bytes 229376 | tf_op jit(solution)/shard_map/all_to_all | solution.py:122
  117.8 0.6 convert_reduce_fusion
  (5 shorter events, 0.1 us)
Async XLA Ops:
  0.0 7.7 %copy-start.2 = (s32[128,2]{0,1:T(2,128)S(1)}, s32[128,2]{0,1:T(2,128)}, u32[]{:S(2)}) copy-start(s32[128,2]{0,1:T(2,128)} %param.7) | copy-start | bytes 3076
  0.0 8.2 %copy-start.1 = (f32[128,2]{0,1:T(2,128)S(1)}, f32[128,2]{0,1:T(2,128)}, u32[]{:S(2)}) copy-start(f32[128,2]{0,1:T(2,128)} %param.6) | copy-start | bytes 3076
  0.0 8.2 %copy-start = (bf16[128,2048]{1,0:T(8,128)(2,1)S(1)}, bf16[128,2048]{1,0:T(8,128)(2,1)}, u32[]{:S(2)}) copy-start(bf16[128,2048]{1,0:T(8,128)(2,1)} %param.5) | copy-start | bytes 1572868
  5.8 30.0 %collective-permute-start = (bf16[3584,256]{1,0:T(8,128)(2,1)}, bf16[3584,256]{1,0:T(8,128)(2,1)}, u32[]{:S(2)}, u32[]{:S(2)}) collective-permute-start(bf16[3584,256]{1,0:T(8,128)(2,1)} %get-tuple-element.8), channel_id=1, source_target_pairs={{0,8},{8,0},{1,9},{9,1},{2,10},{10,2},{3,11},{11,3},{4,12},{12,4},... | collective-permute-start | bytes 5505032 | tf_op jit(solution)/shard_map/ppermute | solution.py:102
  32.6 3.2 %collective-permute-start.1 = (bf16[256,256]{1,0:T(8,128)(2,1)S(1)}, bf16[256,256]{1,0:T(8,128)(2,1)S(1)}, u32[]{:S(2)}, u32[]{:S(2)}) collective-permute-start(bf16[256,256]{1,0:T(8,128)(2,1)S(1)} %bitcast.18), channel_id=1, source_target_pairs={{0,8},{8,0},{1,9},{9,1},{2,10},{10,2},{3,11},{11,3},{4,12},{12,4},... | collective-permute-start | bytes 393224 | tf_op jit(solution)/shard_map/ppermute | solution.py:114

commit v3 on v2

--- a/solution.py
+++ b/solution.py
@@ -70,6 +70,42 @@
     )(core.reshape(1), gate_pre, up_pre)
 
 
+def routed_kernel(tokens_ref, weight_ref, routes_ref, outgoing_ref):
+    groups, capacity, width = outgoing_ref.shape
+    count = tokens_ref.shape[0]
+    named = routes_ref[...] == 0
+    marked = jnp.max(named.astype(jnp.float32), axis=0, keepdims=True)
+    weight = jnp.sum(jnp.where(named, weight_ref[...], 0.0), axis=0, keepdims=True)
+    earlier = lax.broadcasted_iota(jnp.int32, (count, count), 0)
+    later = lax.broadcasted_iota(jnp.int32, (count, count), 1)
+    before = (earlier < later).astype(jnp.bfloat16)
+    position = jnp.dot(
+        jnp.broadcast_to(marked, (8, count)).astype(jnp.bfloat16),
+        before,
+        preferred_element_type=jnp.float32,
+    )[:1]
+    slots = lax.broadcasted_iota(jnp.int32, (capacity, count), 0)
+    taken = (slots == position.astype(jnp.int32)) & (marked > 0.5)
+    chosen = taken.astype(jnp.bfloat16)
+    scale = jnp.sum(jnp.where(taken, weight, 0.0), axis=1, keepdims=True)
+    picked = jnp.dot(chosen, tokens_ref[...], preferred_element_type=jnp.float32)
+    picked = (picked * scale).astype(jnp.bfloat16)
+    for group in range(groups):
+        outgoing_ref[group] = picked[:, group * width : (group + 1) * width]
+
+
+def routed(tokens, weight, routes, groups, capacity):
+    width = tokens.shape[1] // groups
+    return pl.pallas_call(
+        routed_kernel,
+        in_specs=[pl.BlockSpec(memory_space=pltpu.VMEM)] * 3,
+        out_specs=pl.BlockSpec(memory_space=pltpu.VMEM),
+        out_shape=jax.ShapeDtypeStruct((groups, capacity, width), jnp.bfloat16),
+        compiler_params=pltpu.CompilerParams(vmem_limit_bytes=16 << 20),
+        name="routed",
+    )(tokens, weight.T, routes.T)
+
+
 def sum_kernel(terms_ref, sum_ref):
     total = terms_ref[0].astype(jnp.float32)
     for index in range(1, terms_ref.shape[0]):
@@ -98,19 +134,13 @@
     block = units // (planes * fars * 2)
     core = lax.axis_index("core")
 
+    outgoing = routed(d_out, router_weight, routes, group_count, capacity)
+    core, outgoing = lax.optimization_barrier((core, outgoing))
     mine, theirs = hidden_halves(core, gate_pre, up_pre, block)
+    incoming = lax.all_to_all(outgoing, "expert", split_axis=0, concat_axis=0, tiled=True)
+    incoming = incoming.reshape(rows, width)
+    theirs, incoming = lax.optimization_barrier((theirs, incoming))
     met = lax.ppermute(theirs, "core", SWAP)
-
-    named = routes == 0
-    marked = jnp.any(named, axis=1)
-    weight = jnp.sum(jnp.where(named, router_weight, 0.0), axis=1)
-    count = marked.astype(jnp.int32)
-    position = jnp.cumsum(count, dtype=jnp.int32) - count
-    slots = lax.broadcasted_iota(jnp.int32, (capacity, d_out.shape[0]), 0)
-    chosen = ((slots == position[None, :]) & marked[None, :]).astype(jnp.bfloat16)
-    scaled = (d_out.astype(jnp.float32) * weight[:, None]).astype(jnp.bfloat16)
-    outgoing = jnp.dot(chosen, scaled, preferred_element_type=jnp.float32).astype(jnp.bfloat16)
-    incoming = lax.all_to_all(outgoing, "expert", split_axis=1, concat_axis=0, tiled=True)
     incoming_met = lax.ppermute(incoming, "core", SWAP)
 
     partial = jnp.dot(mine, incoming, preferred_element_type=jnp.float32) + jnp.dot(

time: 119 us -> 114 us (0.958)
  blocking collectives: 104 us -> 79.4 us
  starting transfers between devices: 3.83 us -> 16.9 us
  waiting for transfers between devices: 0.67 us -> 6.35 us
  local copies, waits for them, and re-layouts: 0.14 us -> 2.4 us
  matrix products: 3.08 us -> 1.27 us
    all_to_all x1 -> x0, blocking collectives: 24.1 us -> none  [body(): lax.all_to_all(outgoing, 'expert', split_axis=1, concat_axis=0, tiled=True)]
    all_to_all x0 -> x1, starting transfers between devices: none -> 12.6 us  [body(): lax.all_to_all(outgoing, 'expert', split_axis=0, concat_axis=0, tiled=True)]
    all_to_all x0 -> x1, waiting for transfers between devices: none -> 5.43 us  [body(): lax.all_to_all(outgoing, 'expert', split_axis=0, concat_axis=0, tiled=True)]
    unnamed x6, local copies, waits for them, and re-layouts: 0.01 us -> 2.4 us
    dot_general x1, matrix products: 2.15 us -> 0.64 us  [body(): jnp.dot(met, incoming_met, preferred_element_type=jnp.float32)]
  transfers between devices with their start and end apart: 2 -> 3, of which waited for: 1 -> 2; matrix products, arithmetic and copies ran while one was open for 1% -> 1% of each run, Pallas kernels for 0% -> 5%
where the time goes in v3:
time: 114 us
  blocking collectives  79.4 us (70%)
  starting transfers between devices  16.9 us (15%)
  Pallas kernels  6.95 us (6%)
  waiting for transfers between devices  6.35 us (6%)
  local copies, waits for them, and re-layouts  2.4 us (2%)
  matrix products  1.27 us (1%)
    all_to_all x1, blocking collectives, body(): lax.all_to_all(partial, 'far', split_axis=0, concat_axis=0, tiled=True)  48.2 us
    all_to_all x1, blocking collectives, body(): lax.all_to_all(partial, ('x', 'y'), split_axis=0, concat_axis=0, tiled=True)  31.2 us
    all_to_all x1, starting transfers between devices, body(): lax.all_to_all(outgoing, 'expert', split_axis=0, concat_axis=0, tiled=True)  12.6 us
    pallas_call x1, Pallas kernels, hidden_halves(): pl.pallas_call(functools.partial(hidden_kernel, block), in_specs=[pl.Bloc...  5.72 us
    all_to_all x1, waiting for transfers between devices, body(): lax.all_to_all(outgoing, 'expert', split_axis=0, concat_axis=0, tiled=True)  5.43 us
    ppermute x1, starting transfers between devices, body(): incoming_met = lax.ppermute(incoming, 'core', SWAP)  2.41 us
    unnamed x6, local copies, waits for them, and re-layouts  2.4 us
  transfers between devices with their start and end apart: 3, of which 2 were waited for; matrix products, arithmetic and copies ran while one was open for 1% of the time, Pallas kernels for 5%

profile of v3, /device:TPU:34, one launch (start us, length us, event | category | flops | bytes accessed | tf_op | source)
XLA Modules:
  0.0 114.0 jit_solution(4086128888564785774)
XLA Ops:
  0.0 0.0 copy-start
  0.0 1.0 copy-done
  1.0 0.0 copy-start.1
  1.0 0.7 copy-done.1
  1.7 0.0 copy-start.2
  1.7 0.7 copy-done.2
  2.4 1.0 routed.1
  3.4 12.6 %all-to-all-start = ((bf16[8,32,256]{2,1,0:T(8,128)(2,1)}), bf16[8,32,256]{2,1,0:T(8,128)(2,1)S(1)}, u32[]{:S(2)}, u32[]{:S(2)}) async-start(bf16[8,32,256]{2,1,0:T(8,128)(2,1)} %routed.1), calls=%async_computation | async-start | bytes 262144 | tf_op jit(solution)/shard_map/all_to_all | solution.py:140
  16.0 5.7 %hidden.1 = (bf16[3584,256]{1,0:T(8,128)(2,1)S(1)}, bf16[3584,256]{1,0:T(8,128)(2,1)}) custom-call(s32[1]{0:T(128)} %bitcast.2.core_ref, bf16[256,7168]{1,0:T(8,128)(2,1)} %gate_ref.1, bf16[256,7168]{1,0:T(8,128)(2,1)} %up_ref.1), custom_call_target="tpu_custom_call" | custom-call | flops 14680064 | bytes 11010048 | tf_op jit(solution)/shard_map/hidden/pallas_call | solution.py:55
  21.8 5.4 %all-to-all-done = bf16[8,32,256]{2,1,0:T(8,128)(2,1)S(1)} async-done(((bf16[8,32,256]{2,1,0:T(8,128)(2,1)}), bf16[8,32,256]{2,1,0:T(8,128)(2,1)S(1)}, u32[]{:S(2)}, u32[]{:S(2)}) %all-to-all-start) | async-done | bytes 131104 | tf_op jit(solution)/shard_map/all_to_all | solution.py:140
  27.2 1.9 %collective-permute-start = (bf16[3584,256]{1,0:T(8,128)(2,1)}, bf16[3584,256]{1,0:T(8,128)(2,1)S(1)}, u32[]{:S(2)}, u32[]{:S(2)}) collective-permute-start(bf16[3584,256]{1,0:T(8,128)(2,1)} %get-tuple-element.16), channel_id=1, source_target_pairs={{0,8},{8,0},{1,9},{9,1},{2,10},{10,2},{3,11},{11,3},{4,12},{12,4},... | collective-permute-start | bytes 5505032 | tf_op jit(solution)/shard_map/ppermute | solution.py:143
  29.1 2.4 %collective-permute-start.1 = (bf16[256,256]{1,0:T(8,128)(2,1)S(1)}, bf16[256,256]{1,0:T(8,128)(2,1)S(1)}, u32[]{:S(2)}, u32[]{:S(2)}) collective-permute-start(bf16[256,256]{1,0:T(8,128)(2,1)S(1)} %bitcast.14), channel_id=1, source_target_pairs={{0,8},{8,0},{1,9},{9,1},{2,10},{10,2},{3,11},{11,3},{4,12},{12,4},... | collective-permute-start | bytes 393224 | tf_op jit(solution)/shard_map/ppermute | solution.py:144
  31.5 0.6 fusion.1
  32.2 0.9 collective-permute-done.1
  33.0 0.0 collective-permute-done
  33.1 0.6 fusion
  33.7 31.2 %all_to_all.15.terms_ref = bf16[16,224,256]{2,1,0:T(8,128)(2,1)S(1)} all-to-all(bf16[16,224,256]{2,1,0:T(8,128)(2,1)S(1)} %bitcast.13), channel_id=1, replica_groups=mesh['x'=4,'y'=4,'far'=4,'core'=2,'expert'=8] {'x','y'}, dimensions={0} | all-to-all | bytes 3670016 | tf_op jit(solution)/shard_map/all_to_all | solution.py:150
  64.9 0.2 plane_sum.1
  65.2 48.2 %all_to_all.16 = bf16[4,56,256]{2,1,0:T(8,128)(2,1)S(1)} all-to-all(bf16[4,56,256]{2,1,0:T(8,128)(2,1)S(1)} %bitcast.10), channel_id=1, replica_groups=mesh['x'=4,'y'=4,'far'=4,'core'=2,'expert'=8] {'far'}, dimensions={0} | all-to-all | bytes 229376 | tf_op jit(solution)/shard_map/all_to_all | solution.py:152
  113.4 0.6 convert_reduce_fusion
Async XLA Ops:
  0.0 1.0 copy-start
  1.0 0.7 copy-start.1
  1.7 0.7 copy-start.2
  3.4 23.8 %all-to-all-start = ((bf16[8,32,256]{2,1,0:T(8,128)(2,1)}), bf16[8,32,256]{2,1,0:T(8,128)(2,1)S(1)}, u32[]{:S(2)}, u32[]{:S(2)}) async-start(bf16[8,32,256]{2,1,0:T(8,128)(2,1)} %routed.1), calls=%async_computation | async-start | bytes 262144 | tf_op jit(solution)/shard_map/all_to_all | solution.py:140
  27.2 5.9 %collective-permute-start = (bf16[3584,256]{1,0:T(8,128)(2,1)}, bf16[3584,256]{1,0:T(8,128)(2,1)S(1)}, u32[]{:S(2)}, u32[]{:S(2)}) collective-permute-start(bf16[3584,256]{1,0:T(8,128)(2,1)} %get-tuple-element.16), channel_id=1, source_target_pairs={{0,8},{8,0},{1,9},{9,1},{2,10},{10,2},{3,11},{11,3},{4,12},{12,4},... | collective-permute-start | bytes 5505032 | tf_op jit(solution)/shard_map/ppermute | solution.py:143
  29.1 3.9 %collective-permute-start.1 = (bf16[256,256]{1,0:T(8,128)(2,1)S(1)}, bf16[256,256]{1,0:T(8,128)(2,1)S(1)}, u32[]{:S(2)}, u32[]{:S(2)}) collective-permute-start(bf16[256,256]{1,0:T(8,128)(2,1)S(1)} %bitcast.14), channel_id=1, source_target_pairs={{0,8},{8,0},{1,9},{9,1},{2,10},{10,2},{3,11},{11,3},{4,12},{12,4},... | collective-permute-start | bytes 393224 | tf_op jit(solution)/shard_map/ppermute | solution.py:144

commit v4 on v3

--- a/solution.py
+++ b/solution.py
@@ -70,9 +70,24 @@
     )(core.reshape(1), gate_pre, up_pre)
 
 
-def routed_kernel(tokens_ref, weight_ref, routes_ref, outgoing_ref):
+def routed_kernel(tokens_from, weight_from, routes_from, outgoing_ref, *scratch):
+    tokens_ref, weight_ref, routes_ref, sems = scratch
+    copies = [
+        pltpu.make_async_copy(source, target, sems.at[index])
+        for index, (source, target) in enumerate(
+            (
+                (tokens_from, tokens_ref),
+                (weight_from, weight_ref),
+                (routes_from, routes_ref),
+            )
+        )
+    ]
+    for copy in copies:
+        copy.start()
     groups, capacity, width = outgoing_ref.shape
     count = tokens_ref.shape[0]
+    copies[2].wait()
+    copies[1].wait()
     named = routes_ref[...] == 0
     marked = jnp.max(named.astype(jnp.float32), axis=0, keepdims=True)
     weight = jnp.sum(jnp.where(named, weight_ref[...], 0.0), axis=0, keepdims=True)
@@ -88,6 +103,7 @@
     taken = (slots == position.astype(jnp.int32)) & (marked > 0.5)
     chosen = taken.astype(jnp.bfloat16)
     scale = jnp.sum(jnp.where(taken, weight, 0.0), axis=1, keepdims=True)
+    copies[0].wait()
     picked = jnp.dot(chosen, tokens_ref[...], preferred_element_type=jnp.float32)
     picked = (picked * scale).astype(jnp.bfloat16)
     for group in range(groups):
@@ -98,30 +114,46 @@
     width = tokens.shape[1] // groups
     return pl.pallas_call(
         routed_kernel,
-        in_specs=[pl.BlockSpec(memory_space=pltpu.VMEM)] * 3,
+        in_specs=[pl.BlockSpec(memory_space=pl.ANY)] * 3,
         out_specs=pl.BlockSpec(memory_space=pltpu.VMEM),
         out_shape=jax.ShapeDtypeStruct((groups, capacity, width), jnp.bfloat16),
-        compiler_params=pltpu.CompilerParams(vmem_limit_bytes=16 << 20),
+        scratch_shapes=[
+            pltpu.VMEM(tokens.shape, tokens.dtype),
+            pltpu.VMEM(weight.shape[::-1], weight.dtype),
+            pltpu.VMEM(routes.shape[::-1], routes.dtype),
+            pltpu.SemaphoreType.DMA((3,)),
+        ],
+        compiler_params=pltpu.CompilerParams(vmem_limit_bytes=62 << 20),
         name="routed",
     )(tokens, weight.T, routes.T)
 
 
-def sum_kernel(terms_ref, sum_ref):
+def sum_kernel(order_ref, terms_ref, own_ref, passed_ref, sent_ref, total_ref):
     total = terms_ref[0].astype(jnp.float32)
     for index in range(1, terms_ref.shape[0]):
         total = total + terms_ref[index].astype(jnp.float32)
-    sum_ref[...] = total.astype(jnp.bfloat16)
-
-
-def summed(terms):
+    total_ref[...] = total.reshape(total_ref.shape)
+    own_ref[...] = total_ref[order_ref[0]]
+    passed_ref[...] = total_ref[order_ref[1]]
+    sent = jnp.concatenate([total_ref[order_ref[2]], total_ref[order_ref[3]]], axis=0)
+    sent_ref[...] = sent.astype(jnp.bfloat16)
+
+
+def summed(order, terms, fars):
+    block, width = terms.shape[1] // fars, terms.shape[2]
+    piece = jax.ShapeDtypeStruct((block, width), jnp.float32)
     return pl.pallas_call(
         sum_kernel,
-        in_specs=[pl.BlockSpec(memory_space=pltpu.VMEM)],
-        out_specs=pl.BlockSpec(memory_space=pltpu.VMEM),
-        out_shape=jax.ShapeDtypeStruct(terms.shape[1:], jnp.bfloat16),
+        in_specs=[
+            pl.BlockSpec(memory_space=pltpu.SMEM),
+            pl.BlockSpec(memory_space=pltpu.VMEM),
+        ],
+        out_specs=[pl.BlockSpec(memory_space=pltpu.VMEM)] * 3,
+        out_shape=[piece, piece, jax.ShapeDtypeStruct((2 * block, width), jnp.bfloat16)],
+        scratch_shapes=[pltpu.VMEM((fars, block, width), jnp.float32)],
         compiler_params=pltpu.CompilerParams(vmem_limit_bytes=16 << 20),
         name="plane_sum",
-    )(terms)
+    )(order, terms)
 
 
 def body(d_out, router_weight, routes, gate_pre, up_pre):
@@ -135,7 +167,9 @@
     core = lax.axis_index("core")
 
     outgoing = routed(d_out, router_weight, routes, group_count, capacity)
-    core, outgoing = lax.optimization_barrier((core, outgoing))
+    far = lax.axis_index("far")
+    order = jnp.stack([far, far ^ 3, far ^ 1, far ^ 2])
+    core, order, outgoing = lax.optimization_barrier((core, order, outgoing))
     mine, theirs = hidden_halves(core, gate_pre, up_pre, block)
     incoming = lax.all_to_all(outgoing, "expert", split_axis=0, concat_axis=0, tiled=True)
     incoming = incoming.reshape(rows, width)
@@ -148,9 +182,11 @@
     )
     partial = partial.astype(jnp.bfloat16).reshape(planes, fars * block, width)
     partial = lax.all_to_all(partial, ("x", "y"), split_axis=0, concat_axis=0, tiled=True)
-    partial = summed(partial).reshape(fars, block, width)
-    partial = lax.all_to_all(partial, "far", split_axis=0, concat_axis=0, tiled=True)
-    return jnp.sum(partial.astype(jnp.float32), axis=0)
+    own, passed, sent = summed(order, partial, fars)
+    sent = lax.ppermute(sent, "far", [(i, i ^ 1) for i in range(fars)]).astype(jnp.float32)
+    passed = (passed + sent[block:]).astype(jnp.bfloat16)
+    passed = lax.ppermute(passed, "far", [(i, i ^ 3) for i in range(fars)])
+    return own + sent[:block] + passed.astype(jnp.float32)
 
 
 def solution(mesh):

time: 114 us -> 107 us (0.939)
  the two profiles are of different devices: /device:TPU:34 before, /device:TPU:1 now
where the time goes in v4:
time: 107 us; the launch traced here: 106 us
  starting transfers between devices  44.9 us (42%)
  blocking collectives  28.2 us (26%)
  waiting for transfers between devices  22.6 us (21%)
  Pallas kernels  8.6 us (8%)
  matrix products  1.28 us (1%)
    all_to_all x1, blocking collectives, body(): lax.all_to_all(partial, ('x', 'y'), split_axis=0, concat_axis=0, tiled=True)  28.2 us
    ppermute x1, starting transfers between devices, body(): lax.ppermute(sent, 'far', [(i, i ^ 1) for i in range(fars)])  15.4 us
    all_to_all x1, starting transfers between devices, body(): lax.all_to_all(outgoing, 'expert', split_axis=0, concat_axis=0, tiled=True)  13.1 us
    ppermute x1, waiting for transfers between devices, body(): lax.ppermute(sent, 'far', [(i, i ^ 1) for i in range(fars)])  10.8 us
    ppermute x1, starting transfers between devices, body(): met = lax.ppermute(theirs, 'core', SWAP)  7.44 us
    ppermute x1, starting transfers between devices, body(): passed = lax.ppermute(passed, 'far', [(i, i ^ 3) for i in range(fars)])  7.05 us
    ppermute x1, waiting for transfers between devices, body(): passed = lax.ppermute(passed, 'far', [(i, i ^ 3) for i in range(fars)])  6.27 us
    pallas_call x1, Pallas kernels, hidden_halves(): pl.pallas_call(functools.partial(hidden_kernel, block), in_specs=[pl.Bloc...  5.74 us
  transfers between devices with their start and end apart: 5, of which 4 were waited for; matrix products, arithmetic and copies ran while one was open for 1% of the time, Pallas kernels for 5%

profile of v4, /device:TPU:1, one launch (start us, length us, event | category | flops | bytes accessed | tf_op | source)
XLA Modules:
  0.0 106.4 jit_solution(2735660466198399256)
XLA Ops:
  0.0 2.0 %routed.1 = bf16[8,32,256]{2,1,0:T(8,128)(2,1)} custom-call(bf16[128,2048]{1,0:T(8,128)(2,1)} %tokens_from.1, f32[2,128]{1,0:T(2,128)} %bitcast.16, s32[2,128]{1,0:T(2,128)} %bitcast.17), custom_call_target="tpu_custom_call" | custom-call | tf_op jit(solution)/shard_map/routed/pallas_call | solution.py:115
  2.0 0.1 pad_add_fusion.order_ref
  2.1 13.1 %all-to-all-start = ((bf16[8,32,256]{2,1,0:T(8,128)(2,1)}), bf16[8,32,256]{2,1,0:T(8,128)(2,1)S(1)}, u32[]{:S(2)}, u32[]{:S(2)}) async-start(bf16[8,32,256]{2,1,0:T(8,128)(2,1)} %routed.1), calls=%async_computation | async-start | bytes 262144 | tf_op jit(solution)/shard_map/all_to_all | solution.py:174
  15.1 5.7 %hidden.1 = (bf16[3584,256]{1,0:T(8,128)(2,1)S(1)}, bf16[3584,256]{1,0:T(8,128)(2,1)}) custom-call(s32[1]{0:T(128)} %bitcast.6.core_ref, bf16[256,7168]{1,0:T(8,128)(2,1)} %gate_ref.1, bf16[256,7168]{1,0:T(8,128)(2,1)} %up_ref.1), custom_call_target="tpu_custom_call" | custom-call | flops 14680064 | bytes 11010048 | tf_op jit(solution)/shard_map/hidden/pallas_call | solution.py:55
  20.9 4.5 %all-to-all-done = bf16[8,32,256]{2,1,0:T(8,128)(2,1)S(1)} async-done(((bf16[8,32,256]{2,1,0:T(8,128)(2,1)}), bf16[8,32,256]{2,1,0:T(8,128)(2,1)S(1)}, u32[]{:S(2)}, u32[]{:S(2)}) %all-to-all-start) | async-done | bytes 131104 | tf_op jit(solution)/shard_map/all_to_all | solution.py:174
  25.4 7.4 %collective-permute-start = (bf16[3584,256]{1,0:T(8,128)(2,1)}, bf16[3584,256]{1,0:T(8,128)(2,1)S(1)}, u32[]{:S(2)}, u32[]{:S(2)}) collective-permute-start(bf16[3584,256]{1,0:T(8,128)(2,1)} %get-tuple-element.21), channel_id=1, source_target_pairs={{0,8},{8,0},{1,9},{9,1},{2,10},{10,2},{3,11},{11,3},{4,12},{12,4},... | collective-permute-start | bytes 5505032 | tf_op jit(solution)/shard_map/ppermute | solution.py:177
  32.9 1.9 %collective-permute-start.1 = (bf16[256,256]{1,0:T(8,128)(2,1)S(1)}, bf16[256,256]{1,0:T(8,128)(2,1)S(1)}, u32[]{:S(2)}, u32[]{:S(2)}) collective-permute-start(bf16[256,256]{1,0:T(8,128)(2,1)S(1)} %bitcast.14), channel_id=1, source_target_pairs={{0,8},{8,0},{1,9},{9,1},{2,10},{10,2},{3,11},{11,3},{4,12},{12,4},... | collective-permute-start | bytes 393224 | tf_op jit(solution)/shard_map/ppermute | solution.py:178
  34.8 0.6 fusion.3
  35.4 1.0 collective-permute-done.1
  36.4 0.0 collective-permute-done
  36.5 0.6 fusion
  37.1 28.2 %all_to_all.10.terms_ref = bf16[16,224,256]{2,1,0:T(8,128)(2,1)S(1)} all-to-all(bf16[16,224,256]{2,1,0:T(8,128)(2,1)S(1)} %bitcast.13), channel_id=1, replica_groups=mesh['x'=4,'y'=4,'far'=4,'core'=2,'expert'=8] {'x','y'}, dimensions={0} | all-to-all | bytes 3670016 | tf_op jit(solution)/shard_map/all_to_all | solution.py:184
  65.3 0.9 plane_sum.1
  66.2 15.4 %collective-permute-start.2 = (bf16[112,256]{1,0:T(8,128)(2,1)S(1)}, bf16[112,256]{1,0:T(8,128)(2,1)S(1)}, u32[]{:S(2)}, u32[]{:S(2)}) collective-permute-start(bf16[112,256]{1,0:T(8,128)(2,1)S(1)} %get-tuple-element.23), channel_id=1, source_target_pairs={{0,16},{16,0},{32,48},{48,32},{1,17},{17,1},{33,49},{49,33},{2,18}... | collective-permute-start | bytes 172040 | tf_op jit(solution)/shard_map/ppermute | solution.py:186
  81.6 10.8 %collective-permute-done.2 = bf16[112,256]{1,0:T(8,128)(2,1)S(1)} collective-permute-done((bf16[112,256]{1,0:T(8,128)(2,1)S(1)}, bf16[112,256]{1,0:T(8,128)(2,1)S(1)}, u32[]{:S(2)}, u32[]{:S(2)}) %collective-permute-start.2) | collective-permute-done | bytes 57376 | tf_op jit(solution)/shard_map/ppermute | solution.py:186
  92.4 7.1 %collective-permute-start.3 = (bf16[56,256]{1,0:T(8,128)(2,1)S(1)}, bf16[56,256]{1,0:T(8,128)(2,1)S(1)}, u32[]{:S(2)}, u32[]{:S(2)}) collective-permute-start(bf16[56,256]{1,0:T(8,128)(2,1)S(1)} %fusion.1), channel_id=1, source_target_pairs={{0,48},{16,32},{32,16},{48,0},{1,49},{17,33},{33,17},{49,1},{2,50}... | collective-permute-start | bytes 86024 | tf_op jit(solution)/shard_map/ppermute | solution.py:188
  99.5 6.3 %collective-permute-done.3 = bf16[56,256]{1,0:T(8,128)(2,1)S(1)} collective-permute-done((bf16[56,256]{1,0:T(8,128)(2,1)S(1)}, bf16[56,256]{1,0:T(8,128)(2,1)S(1)}, u32[]{:S(2)}, u32[]{:S(2)}) %collective-permute-start.3) | collective-permute-done | bytes 28704 | tf_op jit(solution)/shard_map/ppermute | solution.py:188
  105.8 0.6 fusion.2
  (2 shorter events, 0.0 us)
Async XLA Ops:
  2.1 23.4 %all-to-all-start = ((bf16[8,32,256]{2,1,0:T(8,128)(2,1)}), bf16[8,32,256]{2,1,0:T(8,128)(2,1)S(1)}, u32[]{:S(2)}, u32[]{:S(2)}) async-start(bf16[8,32,256]{2,1,0:T(8,128)(2,1)} %routed.1), calls=%async_computation | async-start | bytes 262144 | tf_op jit(solution)/shard_map/all_to_all | solution.py:174
  25.4 11.0 %collective-permute-start = (bf16[3584,256]{1,0:T(8,128)(2,1)}, bf16[3584,256]{1,0:T(8,128)(2,1)S(1)}, u32[]{:S(2)}, u32[]{:S(2)}) collective-permute-start(bf16[3584,256]{1,0:T(8,128)(2,1)} %get-tuple-element.21), channel_id=1, source_target_pairs={{0,8},{8,0},{1,9},{9,1},{2,10},{10,2},{3,11},{11,3},{4,12},{12,4},... | collective-permute-start | bytes 5505032 | tf_op jit(solution)/shard_map/ppermute | solution.py:177
  32.9 3.6 %collective-permute-start.1 = (bf16[256,256]{1,0:T(8,128)(2,1)S(1)}, bf16[256,256]{1,0:T(8,128)(2,1)S(1)}, u32[]{:S(2)}, u32[]{:S(2)}) collective-permute-start(bf16[256,256]{1,0:T(8,128)(2,1)S(1)} %bitcast.14), channel_id=1, source_target_pairs={{0,8},{8,0},{1,9},{9,1},{2,10},{10,2},{3,11},{11,3},{4,12},{12,4},... | collective-permute-start | bytes 393224 | tf_op jit(solution)/shard_map/ppermute | solution.py:178
  66.2 26.2 %collective-permute-start.2 = (bf16[112,256]{1,0:T(8,128)(2,1)S(1)}, bf16[112,256]{1,0:T(8,128)(2,1)S(1)}, u32[]{:S(2)}, u32[]{:S(2)}) collective-permute-start(bf16[112,256]{1,0:T(8,128)(2,1)S(1)} %get-tuple-element.23), channel_id=1, source_target_pairs={{0,16},{16,0},{32,48},{48,32},{1,17},{17,1},{33,49},{49,33},{2,18}... | collective-permute-start | bytes 172040 | tf_op jit(solution)/shard_map/ppermute | solution.py:186
  92.4 13.3 %collective-permute-start.3 = (bf16[56,256]{1,0:T(8,128)(2,1)S(1)}, bf16[56,256]{1,0:T(8,128)(2,1)S(1)}, u32[]{:S(2)}, u32[]{:S(2)}) collective-permute-start(bf16[56,256]{1,0:T(8,128)(2,1)S(1)} %fusion.1), channel_id=1, source_target_pairs={{0,48},{16,32},{32,16},{48,0},{1,49},{17,33},{33,17},{49,1},{2,50}... | collective-permute-start | bytes 86024 | tf_op jit(solution)/shard_map/ppermute | solution.py:188

commit v5 on v4

--- a/solution.py
+++ b/solution.py
@@ -76,9 +76,9 @@
         pltpu.make_async_copy(source, target, sems.at[index])
         for index, (source, target) in enumerate(
             (
+                (routes_from, routes_ref),
+                (weight_from, weight_ref),
                 (tokens_from, tokens_ref),
-                (weight_from, weight_ref),
-                (routes_from, routes_ref),
             )
         )
     ]
@@ -86,24 +86,24 @@
         copy.start()
     groups, capacity, width = outgoing_ref.shape
     count = tokens_ref.shape[0]
-    copies[2].wait()
+    earlier = lax.broadcasted_iota(jnp.int32, (count, count), 0)
+    later = lax.broadcasted_iota(jnp.int32, (count, count), 1)
+    before = (earlier < later).astype(jnp.bfloat16)
+    slots = lax.broadcasted_iota(jnp.int32, (capacity, count), 0)
+    copies[0].wait()
     copies[1].wait()
     named = routes_ref[...] == 0
     marked = jnp.max(named.astype(jnp.float32), axis=0, keepdims=True)
     weight = jnp.sum(jnp.where(named, weight_ref[...], 0.0), axis=0, keepdims=True)
-    earlier = lax.broadcasted_iota(jnp.int32, (count, count), 0)
-    later = lax.broadcasted_iota(jnp.int32, (count, count), 1)
-    before = (earlier < later).astype(jnp.bfloat16)
     position = jnp.dot(
         jnp.broadcast_to(marked, (8, count)).astype(jnp.bfloat16),
         before,
         preferred_element_type=jnp.float32,
     )[:1]
-    slots = lax.broadcasted_iota(jnp.int32, (capacity, count), 0)
     taken = (slots == position.astype(jnp.int32)) & (marked > 0.5)
     chosen = taken.astype(jnp.bfloat16)
     scale = jnp.sum(jnp.where(taken, weight, 0.0), axis=1, keepdims=True)
-    copies[0].wait()
+    copies[2].wait()
     picked = jnp.dot(chosen, tokens_ref[...], preferred_element_type=jnp.float32)
     picked = (picked * scale).astype(jnp.bfloat16)
     for group in range(groups):
@@ -128,18 +128,23 @@
     )(tokens, weight.T, routes.T)
 
 
-def sum_kernel(order_ref, terms_ref, own_ref, passed_ref, sent_ref, total_ref):
+def sum_kernel(far_ref, terms_ref, own_ref, passed_ref, sent_ref):
+    block, width = own_ref.shape
     total = terms_ref[0].astype(jnp.float32)
     for index in range(1, terms_ref.shape[0]):
         total = total + terms_ref[index].astype(jnp.float32)
-    total_ref[...] = total.reshape(total_ref.shape)
-    own_ref[...] = total_ref[order_ref[0]]
-    passed_ref[...] = total_ref[order_ref[1]]
-    sent = jnp.concatenate([total_ref[order_ref[2]], total_ref[order_ref[3]]], axis=0)
-    sent_ref[...] = sent.astype(jnp.bfloat16)
-
-
-def summed(order, terms, fars):
+    total = total.reshape(-1, block, width)
+    for far in range(total.shape[0]):
+
+        @pl.when(far_ref[0] == far)
+        def _():
+            own_ref[...] = total[far]
+            passed_ref[...] = total[far ^ 3]
+            sent = jnp.concatenate([total[far ^ 1], total[far ^ 2]], axis=0)
+            sent_ref[...] = sent.astype(jnp.bfloat16)
+
+
+def summed(far, terms, fars):
     block, width = terms.shape[1] // fars, terms.shape[2]
     piece = jax.ShapeDtypeStruct((block, width), jnp.float32)
     return pl.pallas_call(
@@ -150,10 +155,9 @@
         ],
         out_specs=[pl.BlockSpec(memory_space=pltpu.VMEM)] * 3,
         out_shape=[piece, piece, jax.ShapeDtypeStruct((2 * block, width), jnp.bfloat16)],
-        scratch_shapes=[pltpu.VMEM((fars, block, width), jnp.float32)],
         compiler_params=pltpu.CompilerParams(vmem_limit_bytes=16 << 20),
         name="plane_sum",
-    )(order, terms)
+    )(far.reshape(1), terms)
 
 
 def body(d_out, router_weight, routes, gate_pre, up_pre):
@@ -168,8 +172,7 @@
 
     outgoing = routed(d_out, router_weight, routes, group_count, capacity)
     far = lax.axis_index("far")
-    order = jnp.stack([far, far ^ 3, far ^ 1, far ^ 2])
-    core, order, outgoing = lax.optimization_barrier((core, order, outgoing))
+    core, far, outgoing = lax.optimization_barrier((core, far, outgoing))
     mine, theirs = hidden_halves(core, gate_pre, up_pre, block)
     incoming = lax.all_to_all(outgoing, "expert", split_axis=0, concat_axis=0, tiled=True)
     incoming = incoming.reshape(rows, width)
@@ -182,7 +185,7 @@
     )
     partial = partial.astype(jnp.bfloat16).reshape(planes, fars * block, width)
     partial = lax.all_to_all(partial, ("x", "y"), split_axis=0, concat_axis=0, tiled=True)
-    own, passed, sent = summed(order, partial, fars)
+    own, passed, sent = summed(far, partial, fars)
     sent = lax.ppermute(sent, "far", [(i, i ^ 1) for i in range(fars)]).astype(jnp.float32)
     passed = (passed + sent[block:]).astype(jnp.bfloat16)
     passed = lax.ppermute(passed, "far", [(i, i ^ 3) for i in range(fars)])

time: 107 us -> 106 us (level)
  no operation moved by 1% of the time
where the time goes in v5:
time: 106 us
  starting transfers between devices  45 us (42%)
  blocking collectives  28.1 us (27%)
  waiting for transfers between devices  22.6 us (21%)
  Pallas kernels  8.08 us (8%)
  matrix products  1.26 us (1%)
    all_to_all x1, blocking collectives, body(): lax.all_to_all(partial, ('x', 'y'), split_axis=0, concat_axis=0, tiled=True)  28.1 us
    ppermute x1, starting transfers between devices, body(): lax.ppermute(sent, 'far', [(i, i ^ 1) for i in range(fars)])  15.5 us
    all_to_all x1, starting transfers between devices, body(): lax.all_to_all(outgoing, 'expert', split_axis=0, concat_axis=0, tiled=True)  13.1 us
    ppermute x1, waiting for transfers between devices, body(): lax.ppermute(sent, 'far', [(i, i ^ 1) for i in range(fars)])  10.8 us
    ppermute x1, starting transfers between devices, body(): met = lax.ppermute(theirs, 'core', SWAP)  7.44 us
    ppermute x1, starting transfers between devices, body(): passed = lax.ppermute(passed, 'far', [(i, i ^ 3) for i in range(fars)])  7.04 us
    ppermute x1, waiting for transfers between devices, body(): passed = lax.ppermute(passed, 'far', [(i, i ^ 3) for i in range(fars)])  6.28 us
    pallas_call x1, Pallas kernels, hidden_halves(): pl.pallas_call(functools.partial(hidden_kernel, block), in_specs=[pl.Bloc...  5.74 us
  transfers between devices with their start and end apart: 5, of which 4 were waited for; matrix products, arithmetic and copies ran while one was open for 1% of the time, Pallas kernels for 5%

profile of v5, /device:TPU:1, one launch (start us, length us, event | category | flops | bytes accessed | tf_op | source)
XLA Modules:
  0.0 105.8 jit_solution(5654482133641153653)
XLA Ops:
  0.0 2.0 %routed.1 = bf16[8,32,256]{2,1,0:T(8,128)(2,1)} custom-call(bf16[128,2048]{1,0:T(8,128)(2,1)} %tokens_from.1, f32[2,128]{1,0:T(2,128)} %bitcast.13, s32[2,128]{1,0:T(2,128)} %bitcast.14), custom_call_target="tpu_custom_call" | custom-call | tf_op jit(solution)/shard_map/routed/pallas_call | solution.py:115
  2.0 13.1 %all-to-all-start = ((bf16[8,32,256]{2,1,0:T(8,128)(2,1)}), bf16[8,32,256]{2,1,0:T(8,128)(2,1)S(1)}, u32[]{:S(2)}, u32[]{:S(2)}) async-start(bf16[8,32,256]{2,1,0:T(8,128)(2,1)} %routed.1), calls=%async_computation | async-start | bytes 262144 | tf_op jit(solution)/shard_map/all_to_all | solution.py:177
  15.1 5.7 %hidden.1 = (bf16[3584,256]{1,0:T(8,128)(2,1)S(1)}, bf16[3584,256]{1,0:T(8,128)(2,1)}) custom-call(s32[1]{0:T(128)} %bitcast.3.core_ref, bf16[256,7168]{1,0:T(8,128)(2,1)} %gate_ref.1, bf16[256,7168]{1,0:T(8,128)(2,1)} %up_ref.1), custom_call_target="tpu_custom_call" | custom-call | flops 14680064 | bytes 11010048 | tf_op jit(solution)/shard_map/hidden/pallas_call | solution.py:55
  20.8 4.5 %all-to-all-done = bf16[8,32,256]{2,1,0:T(8,128)(2,1)S(1)} async-done(((bf16[8,32,256]{2,1,0:T(8,128)(2,1)}), bf16[8,32,256]{2,1,0:T(8,128)(2,1)S(1)}, u32[]{:S(2)}, u32[]{:S(2)}) %all-to-all-start) | async-done | bytes 131104 | tf_op jit(solution)/shard_map/all_to_all | solution.py:177
  25.4 7.4 %collective-permute-start = (bf16[3584,256]{1,0:T(8,128)(2,1)}, bf16[3584,256]{1,0:T(8,128)(2,1)S(1)}, u32[]{:S(2)}, u32[]{:S(2)}) collective-permute-start(bf16[3584,256]{1,0:T(8,128)(2,1)} %get-tuple-element.21), channel_id=1, source_target_pairs={{0,8},{8,0},{1,9},{9,1},{2,10},{10,2},{3,11},{11,3},{4,12},{12,4},... | collective-permute-start | bytes 5505032 | tf_op jit(solution)/shard_map/ppermute | solution.py:180
  32.8 1.9 %collective-permute-start.1 = (bf16[256,256]{1,0:T(8,128)(2,1)S(1)}, bf16[256,256]{1,0:T(8,128)(2,1)S(1)}, u32[]{:S(2)}, u32[]{:S(2)}) collective-permute-start(bf16[256,256]{1,0:T(8,128)(2,1)S(1)} %bitcast.11), channel_id=1, source_target_pairs={{0,8},{8,0},{1,9},{9,1},{2,10},{10,2},{3,11},{11,3},{4,12},{12,4},... | collective-permute-start | bytes 393224 | tf_op jit(solution)/shard_map/ppermute | solution.py:181
  34.7 0.6 fusion.3
  35.4 1.0 collective-permute-done.1
  36.4 0.0 collective-permute-done
  36.4 0.6 fusion
  37.0 28.1 %all_to_all.10.terms_ref = bf16[16,224,256]{2,1,0:T(8,128)(2,1)S(1)} all-to-all(bf16[16,224,256]{2,1,0:T(8,128)(2,1)S(1)} %bitcast.10), channel_id=1, replica_groups=mesh['x'=4,'y'=4,'far'=4,'core'=2,'expert'=8] {'x','y'}, dimensions={0} | all-to-all | bytes 3670016 | tf_op jit(solution)/shard_map/all_to_all | solution.py:187
  65.2 0.4 plane_sum.1
  65.6 15.5 %collective-permute-start.2 = (bf16[112,256]{1,0:T(8,128)(2,1)S(1)}, bf16[112,256]{1,0:T(8,128)(2,1)S(1)}, u32[]{:S(2)}, u32[]{:S(2)}) collective-permute-start(bf16[112,256]{1,0:T(8,128)(2,1)S(1)} %get-tuple-element.23), channel_id=1, source_target_pairs={{0,16},{16,0},{32,48},{48,32},{1,17},{17,1},{33,49},{49,33},{2,18}... | collective-permute-start | bytes 172040 | tf_op jit(solution)/shard_map/ppermute | solution.py:189
  81.0 10.8 %collective-permute-done.2 = bf16[112,256]{1,0:T(8,128)(2,1)S(1)} collective-permute-done((bf16[112,256]{1,0:T(8,128)(2,1)S(1)}, bf16[112,256]{1,0:T(8,128)(2,1)S(1)}, u32[]{:S(2)}, u32[]{:S(2)}) %collective-permute-start.2) | collective-permute-done | bytes 57376 | tf_op jit(solution)/shard_map/ppermute | solution.py:189
  91.8 7.0 %collective-permute-start.3 = (bf16[56,256]{1,0:T(8,128)(2,1)S(1)}, bf16[56,256]{1,0:T(8,128)(2,1)S(1)}, u32[]{:S(2)}, u32[]{:S(2)}) collective-permute-start(bf16[56,256]{1,0:T(8,128)(2,1)S(1)} %fusion.1), channel_id=1, source_target_pairs={{0,48},{16,32},{32,16},{48,0},{1,49},{17,33},{33,17},{49,1},{2,50}... | collective-permute-start | bytes 86024 | tf_op jit(solution)/shard_map/ppermute | solution.py:191
  98.9 6.3 %collective-permute-done.3 = bf16[56,256]{1,0:T(8,128)(2,1)S(1)} collective-permute-done((bf16[56,256]{1,0:T(8,128)(2,1)S(1)}, bf16[56,256]{1,0:T(8,128)(2,1)S(1)}, u32[]{:S(2)}, u32[]{:S(2)}) %collective-permute-start.3) | collective-permute-done | bytes 28704 | tf_op jit(solution)/shard_map/ppermute | solution.py:191
  105.2 0.6 fusion.2
  (2 shorter events, 0.0 us)
Async XLA Ops:
  2.0 23.4 %all-to-all-start = ((bf16[8,32,256]{2,1,0:T(8,128)(2,1)}), bf16[8,32,256]{2,1,0:T(8,128)(2,1)S(1)}, u32[]{:S(2)}, u32[]{:S(2)}) async-start(bf16[8,32,256]{2,1,0:T(8,128)(2,1)} %routed.1), calls=%async_computation | async-start | bytes 262144 | tf_op jit(solution)/shard_map/all_to_all | solution.py:177
  25.4 11.0 %collective-permute-start = (bf16[3584,256]{1,0:T(8,128)(2,1)}, bf16[3584,256]{1,0:T(8,128)(2,1)S(1)}, u32[]{:S(2)}, u32[]{:S(2)}) collective-permute-start(bf16[3584,256]{1,0:T(8,128)(2,1)} %get-tuple-element.21), channel_id=1, source_target_pairs={{0,8},{8,0},{1,9},{9,1},{2,10},{10,2},{3,11},{11,3},{4,12},{12,4},... | collective-permute-start | bytes 5505032 | tf_op jit(solution)/shard_map/ppermute | solution.py:180
  32.8 3.6 %collective-permute-start.1 = (bf16[256,256]{1,0:T(8,128)(2,1)S(1)}, bf16[256,256]{1,0:T(8,128)(2,1)S(1)}, u32[]{:S(2)}, u32[]{:S(2)}) collective-permute-start(bf16[256,256]{1,0:T(8,128)(2,1)S(1)} %bitcast.11), channel_id=1, source_target_pairs={{0,8},{8,0},{1,9},{9,1},{2,10},{10,2},{3,11},{11,3},{4,12},{12,4},... | collective-permute-start | bytes 393224 | tf_op jit(solution)/shard_map/ppermute | solution.py:181
  65.6 26.3 %collective-permute-start.2 = (bf16[112,256]{1,0:T(8,128)(2,1)S(1)}, bf16[112,256]{1,0:T(8,128)(2,1)S(1)}, u32[]{:S(2)}, u32[]{:S(2)}) collective-permute-start(bf16[112,256]{1,0:T(8,128)(2,1)S(1)} %get-tuple-element.23), channel_id=1, source_target_pairs={{0,16},{16,0},{32,48},{48,32},{1,17},{17,1},{33,49},{49,33},{2,18}... | collective-permute-start | bytes 172040 | tf_op jit(solution)/shard_map/ppermute | solution.py:189
  91.8 13.3 %collective-permute-start.3 = (bf16[56,256]{1,0:T(8,128)(2,1)S(1)}, bf16[56,256]{1,0:T(8,128)(2,1)S(1)}, u32[]{:S(2)}, u32[]{:S(2)}) collective-permute-start(bf16[56,256]{1,0:T(8,128)(2,1)S(1)} %fusion.1), channel_id=1, source_target_pairs={{0,48},{16,32},{32,16},{48,0},{1,49},{17,33},{33,17},{49,1},{2,50}... | collective-permute-start | bytes 86024 | tf_op jit(solution)/shard_map/ppermute | solution.py:191

commit v6 on v5

--- a/solution.py
+++ b/solution.py
@@ -1,4 +1,5 @@
 import functools
+import itertools
 
 import jax
 import jax.numpy as jnp
@@ -10,6 +11,15 @@
 GRID = (("x", 4), ("y", 4), ("far", 4), ("core", 2))
 SWAP = [(0, 1), (1, 0)]
 PARTS = 8
+PARTNERS = ((1, 3), (3, 1))
+
+
+def mirrored(step, fars):
+    return [
+        (2 * far + core, 2 * (far ^ PARTNERS[step][core]) + core)
+        for far in range(fars)
+        for core in (0, 1)
+    ]
 
 
 def hidden_kernel(block, core_ref, gate_ref, up_ref, mine_ref, theirs_ref, gate, up, sems):
@@ -128,23 +138,23 @@
     )(tokens, weight.T, routes.T)
 
 
-def sum_kernel(far_ref, terms_ref, own_ref, passed_ref, sent_ref):
+def sum_kernel(place_ref, terms_ref, own_ref, passed_ref, sent_ref):
     block, width = own_ref.shape
     total = terms_ref[0].astype(jnp.float32)
     for index in range(1, terms_ref.shape[0]):
         total = total + terms_ref[index].astype(jnp.float32)
     total = total.reshape(-1, block, width)
-    for far in range(total.shape[0]):
-
-        @pl.when(far_ref[0] == far)
+    for place, (far, core) in enumerate(itertools.product(range(total.shape[0]), (0, 1))):
+
+        @pl.when(place_ref[0] == place)
         def _():
             own_ref[...] = total[far]
-            passed_ref[...] = total[far ^ 3]
-            sent = jnp.concatenate([total[far ^ 1], total[far ^ 2]], axis=0)
+            passed_ref[...] = total[far ^ PARTNERS[1][core]]
+            sent = jnp.concatenate([total[far ^ PARTNERS[0][core]], total[far ^ 2]], axis=0)
             sent_ref[...] = sent.astype(jnp.bfloat16)
 
 
-def summed(far, terms, fars):
+def summed(place, terms, fars):
     block, width = terms.shape[1] // fars, terms.shape[2]
     piece = jax.ShapeDtypeStruct((block, width), jnp.float32)
     return pl.pallas_call(
@@ -157,7 +167,7 @@
         out_shape=[piece, piece, jax.ShapeDtypeStruct((2 * block, width), jnp.bfloat16)],
         compiler_params=pltpu.CompilerParams(vmem_limit_bytes=16 << 20),
         name="plane_sum",
-    )(far.reshape(1), terms)
+    )(place.reshape(1), terms)
 
 
 def body(d_out, router_weight, routes, gate_pre, up_pre):
@@ -171,8 +181,8 @@
     core = lax.axis_index("core")
 
     outgoing = routed(d_out, router_weight, routes, group_count, capacity)
-    far = lax.axis_index("far")
-    core, far, outgoing = lax.optimization_barrier((core, far, outgoing))
+    place = lax.axis_index(("far", "core"))
+    core, place, outgoing = lax.optimization_barrier((core, place, outgoing))
     mine, theirs = hidden_halves(core, gate_pre, up_pre, block)
     incoming = lax.all_to_all(outgoing, "expert", split_axis=0, concat_axis=0, tiled=True)
     incoming = incoming.reshape(rows, width)
@@ -185,10 +195,10 @@
     )
     partial = partial.astype(jnp.bfloat16).reshape(planes, fars * block, width)
     partial = lax.all_to_all(partial, ("x", "y"), split_axis=0, concat_axis=0, tiled=True)
-    own, passed, sent = summed(far, partial, fars)
-    sent = lax.ppermute(sent, "far", [(i, i ^ 1) for i in range(fars)]).astype(jnp.float32)
+    own, passed, sent = summed(place, partial, fars)
+    sent = lax.ppermute(sent, ("far", "core"), mirrored(0, fars)).astype(jnp.float32)
     passed = (passed + sent[block:]).astype(jnp.bfloat16)
-    passed = lax.ppermute(passed, "far", [(i, i ^ 3) for i in range(fars)])
+    passed = lax.ppermute(passed, ("far", "core"), mirrored(1, fars))
     return own + sent[:block] + passed.astype(jnp.float32)
 
 

time: 106 us -> 102 us (0.962)
  waiting for transfers between devices: 22.6 us -> 11.8 us
  starting transfers between devices: 45 us -> 51.1 us
    ppermute x2, waiting for transfers between devices: 17.1 us -> 6.21 us  [the longest x1 4.69 us: body(): lax.ppermute(sent, ('far', 'core'), mirrored(0, fars)).astype(jnp.float32)]
    ppermute x2, starting transfers between devices: 22.5 us -> 28.6 us  [the longest x1 15.2 us: body(): lax.ppermute(sent, ('far', 'core'), mirrored(0, fars)).astype(jnp.float32)]
  transfers between devices with their start and end apart: 5 -> 5, of which waited for: 4 -> 4; matrix products, arithmetic and copies ran while one was open for 1% -> 1% of each run, Pallas kernels for 5% -> 6%
where the time goes in v6:
time: 102 us; the launch traced here: 101 us
  starting transfers between devices  51.1 us (50%)
  blocking collectives  28.1 us (28%)
  waiting for transfers between devices  11.8 us (12%)
  Pallas kernels  8.12 us (8%)
  matrix products  1.26 us (1%)
    all_to_all x1, blocking collectives, body(): lax.all_to_all(partial, ('x', 'y'), split_axis=0, concat_axis=0, tiled=True)  28.1 us
    ppermute x1, starting transfers between devices, body(): lax.ppermute(sent, ('far', 'core'), mirrored(0, fars)).astype(jnp.float32)  15.2 us
    ppermute x1, starting transfers between devices, body(): passed = lax.ppermute(passed, ('far', 'core'), mirrored(1, fars))  13.4 us
    all_to_all x1, starting transfers between devices, body(): lax.all_to_all(outgoing, 'expert', split_axis=0, concat_axis=0, tiled=True)  13.1 us
    ppermute x1, starting transfers between devices, body(): met = lax.ppermute(theirs, 'core', SWAP)  7.44 us
    pallas_call x1, Pallas kernels, hidden_halves(): pl.pallas_call(functools.partial(hidden_kernel, block), in_specs=[pl.Bloc...  5.74 us
    ppermute x1, waiting for transfers between devices, body(): lax.ppermute(sent, ('far', 'core'), mirrored(0, fars)).astype(jnp.float32)  4.69 us
    all_to_all x1, waiting for transfers between devices, body(): lax.all_to_all(outgoing, 'expert', split_axis=0, concat_axis=0, tiled=True)  4.53 us
  transfers between devices with their start and end apart: 5, of which 4 were waited for; matrix products, arithmetic and copies ran while one was open for 1% of the time, Pallas kernels for 6%

profile of v6, /device:TPU:1, one launch (start us, length us, event | category | flops | bytes accessed | tf_op | source)
XLA Modules:
  0.0 101.1 jit_solution(13173404968955104174)
XLA Ops:
  0.0 2.0 %routed.1 = bf16[8,32,256]{2,1,0:T(8,128)(2,1)} custom-call(bf16[128,2048]{1,0:T(8,128)(2,1)} %tokens_from.1, f32[2,128]{1,0:T(2,128)} %bitcast.13, s32[2,128]{1,0:T(2,128)} %bitcast.14), custom_call_target="tpu_custom_call" | custom-call | tf_op jit(solution)/shard_map/routed/pallas_call | solution.py:125
  2.0 13.1 %all-to-all-start = ((bf16[8,32,256]{2,1,0:T(8,128)(2,1)}), bf16[8,32,256]{2,1,0:T(8,128)(2,1)S(1)}, u32[]{:S(2)}, u32[]{:S(2)}) async-start(bf16[8,32,256]{2,1,0:T(8,128)(2,1)} %routed.1), calls=%async_computation | async-start | bytes 262144 | tf_op jit(solution)/shard_map/all_to_all | solution.py:187
  15.1 5.7 %hidden.1 = (bf16[3584,256]{1,0:T(8,128)(2,1)S(1)}, bf16[3584,256]{1,0:T(8,128)(2,1)}) custom-call(s32[1]{0:T(128)} %bitcast.3.core_ref, bf16[256,7168]{1,0:T(8,128)(2,1)} %gate_ref.1, bf16[256,7168]{1,0:T(8,128)(2,1)} %up_ref.1), custom_call_target="tpu_custom_call" | custom-call | flops 14680064 | bytes 11010048 | tf_op jit(solution)/shard_map/hidden/pallas_call | solution.py:65
  20.8 4.5 %all-to-all-done = bf16[8,32,256]{2,1,0:T(8,128)(2,1)S(1)} async-done(((bf16[8,32,256]{2,1,0:T(8,128)(2,1)}), bf16[8,32,256]{2,1,0:T(8,128)(2,1)S(1)}, u32[]{:S(2)}, u32[]{:S(2)}) %all-to-all-start) | async-done | bytes 131104 | tf_op jit(solution)/shard_map/all_to_all | solution.py:187
  25.4 7.4 %collective-permute-start = (bf16[3584,256]{1,0:T(8,128)(2,1)}, bf16[3584,256]{1,0:T(8,128)(2,1)S(1)}, u32[]{:S(2)}, u32[]{:S(2)}) collective-permute-start(bf16[3584,256]{1,0:T(8,128)(2,1)} %get-tuple-element.21), channel_id=1, source_target_pairs={{0,8},{8,0},{1,9},{9,1},{2,10},{10,2},{3,11},{11,3},{4,12},{12,4},... | collective-permute-start | bytes 5505032 | tf_op jit(solution)/shard_map/ppermute | solution.py:190
  32.8 1.9 %collective-permute-start.1 = (bf16[256,256]{1,0:T(8,128)(2,1)S(1)}, bf16[256,256]{1,0:T(8,128)(2,1)S(1)}, u32[]{:S(2)}, u32[]{:S(2)}) collective-permute-start(bf16[256,256]{1,0:T(8,128)(2,1)S(1)} %bitcast.11), channel_id=1, source_target_pairs={{0,8},{8,0},{1,9},{9,1},{2,10},{10,2},{3,11},{11,3},{4,12},{12,4},... | collective-permute-start | bytes 393224 | tf_op jit(solution)/shard_map/ppermute | solution.py:191
  34.7 0.6 fusion.3
  35.4 1.0 %collective-permute-done.1 = bf16[256,256]{1,0:T(8,128)(2,1)S(1)} collective-permute-done((bf16[256,256]{1,0:T(8,128)(2,1)S(1)}, bf16[256,256]{1,0:T(8,128)(2,1)S(1)}, u32[]{:S(2)}, u32[]{:S(2)}) %collective-permute-start.1) | collective-permute-done | bytes 131104 | tf_op jit(solution)/shard_map/ppermute | solution.py:191
  36.4 0.0 collective-permute-done
  36.4 0.6 fusion
  37.0 28.1 %all_to_all.10.terms_ref = bf16[16,224,256]{2,1,0:T(8,128)(2,1)S(1)} all-to-all(bf16[16,224,256]{2,1,0:T(8,128)(2,1)S(1)} %bitcast.10), channel_id=1, replica_groups=mesh['x'=4,'y'=4,'far'=4,'core'=2,'expert'=8] {'x','y'}, dimensions={0} | all-to-all | bytes 3670016 | tf_op jit(solution)/shard_map/all_to_all | solution.py:197
  65.2 0.4 plane_sum.1
  65.6 15.2 %collective-permute-start.2 = (bf16[112,256]{1,0:T(8,128)(2,1)S(1)}, bf16[112,256]{1,0:T(8,128)(2,1)S(1)}, u32[]{:S(2)}, u32[]{:S(2)}) collective-permute-start(bf16[112,256]{1,0:T(8,128)(2,1)S(1)} %get-tuple-element.23), channel_id=1, source_target_pairs={{0,16},{8,56},{16,0},{24,40},{32,48},{40,24},{48,32},{56,8},{1,17}... | collective-permute-start | bytes 172040 | tf_op jit(solution)/shard_map/ppermute | solution.py:199
  80.8 4.7 %collective-permute-done.2 = bf16[112,256]{1,0:T(8,128)(2,1)S(1)} collective-permute-done((bf16[112,256]{1,0:T(8,128)(2,1)S(1)}, bf16[112,256]{1,0:T(8,128)(2,1)S(1)}, u32[]{:S(2)}, u32[]{:S(2)}) %collective-permute-start.2) | collective-permute-done | bytes 57376 | tf_op jit(solution)/shard_map/ppermute | solution.py:199
  85.6 13.4 %collective-permute-start.3 = (bf16[56,256]{1,0:T(8,128)(2,1)S(1)}, bf16[56,256]{1,0:T(8,128)(2,1)S(1)}, u32[]{:S(2)}, u32[]{:S(2)}) collective-permute-start(bf16[56,256]{1,0:T(8,128)(2,1)S(1)} %fusion.1), channel_id=1, source_target_pairs={{0,48},{8,24},{16,32},{24,8},{32,16},{40,56},{48,0},{56,40},{1,49}... | collective-permute-start | bytes 86024 | tf_op jit(solution)/shard_map/ppermute | solution.py:201
  98.9 1.5 %collective-permute-done.3 = bf16[56,256]{1,0:T(8,128)(2,1)S(1)} collective-permute-done((bf16[56,256]{1,0:T(8,128)(2,1)S(1)}, bf16[56,256]{1,0:T(8,128)(2,1)S(1)}, u32[]{:S(2)}, u32[]{:S(2)}) %collective-permute-start.3) | collective-permute-done | bytes 28704 | tf_op jit(solution)/shard_map/ppermute | solution.py:201
  100.5 0.6 fusion.2
  (2 shorter events, 0.0 us)
Async XLA Ops:
  2.0 23.4 %all-to-all-start = ((bf16[8,32,256]{2,1,0:T(8,128)(2,1)}), bf16[8,32,256]{2,1,0:T(8,128)(2,1)S(1)}, u32[]{:S(2)}, u32[]{:S(2)}) async-start(bf16[8,32,256]{2,1,0:T(8,128)(2,1)} %routed.1), calls=%async_computation | async-start | bytes 262144 | tf_op jit(solution)/shard_map/all_to_all | solution.py:187
  25.4 11.0 %collective-permute-start = (bf16[3584,256]{1,0:T(8,128)(2,1)}, bf16[3584,256]{1,0:T(8,128)(2,1)S(1)}, u32[]{:S(2)}, u32[]{:S(2)}) collective-permute-start(bf16[3584,256]{1,0:T(8,128)(2,1)} %get-tuple-element.21), channel_id=1, source_target_pairs={{0,8},{8,0},{1,9},{9,1},{2,10},{10,2},{3,11},{11,3},{4,12},{12,4},... | collective-permute-start | bytes 5505032 | tf_op jit(solution)/shard_map/ppermute | solution.py:190
  32.8 3.6 %collective-permute-start.1 = (bf16[256,256]{1,0:T(8,128)(2,1)S(1)}, bf16[256,256]{1,0:T(8,128)(2,1)S(1)}, u32[]{:S(2)}, u32[]{:S(2)}) collective-permute-start(bf16[256,256]{1,0:T(8,128)(2,1)S(1)} %bitcast.11), channel_id=1, source_target_pairs={{0,8},{8,0},{1,9},{9,1},{2,10},{10,2},{3,11},{11,3},{4,12},{12,4},... | collective-permute-start | bytes 393224 | tf_op jit(solution)/shard_map/ppermute | solution.py:191
  65.6 19.9 %collective-permute-start.2 = (bf16[112,256]{1,0:T(8,128)(2,1)S(1)}, bf16[112,256]{1,0:T(8,128)(2,1)S(1)}, u32[]{:S(2)}, u32[]{:S(2)}) collective-permute-start(bf16[112,256]{1,0:T(8,128)(2,1)S(1)} %get-tuple-element.23), channel_id=1, source_target_pairs={{0,16},{8,56},{16,0},{24,40},{32,48},{40,24},{48,32},{56,8},{1,17}... | collective-permute-start | bytes 172040 | tf_op jit(solution)/shard_map/ppermute | solution.py:199
  85.6 14.9 %collective-permute-start.3 = (bf16[56,256]{1,0:T(8,128)(2,1)S(1)}, bf16[56,256]{1,0:T(8,128)(2,1)S(1)}, u32[]{:S(2)}, u32[]{:S(2)}) collective-permute-start(bf16[56,256]{1,0:T(8,128)(2,1)S(1)} %fusion.1), channel_id=1, source_target_pairs={{0,48},{8,24},{16,32},{24,8},{32,16},{40,56},{48,0},{56,40},{1,49}... | collective-permute-start | bytes 86024 | tf_op jit(solution)/shard_map/ppermute | solution.py:201

commit v7 on v6

--- a/solution.py
+++ b/solution.py
@@ -11,7 +11,7 @@
 GRID = (("x", 4), ("y", 4), ("far", 4), ("core", 2))
 SWAP = [(0, 1), (1, 0)]
 PARTS = 8
-PARTNERS = ((1, 3), (3, 1))
+PARTNERS = ((3, 1), (1, 3))
 
 
 def mirrored(step, fars):

time: 102 us -> 102 us (level)
  starting transfers between devices: 51.1 us -> 45.6 us
  waiting for transfers between devices: 11.8 us -> 17.1 us
    ppermute x1, starting transfers between devices: 13.4 us -> 7.64 us  [body(): passed = lax.ppermute(passed, ('far', 'core'), mirrored(1, fars))]
    ppermute x1, waiting for transfers between devices: 1.52 us -> 5.68 us  [body(): passed = lax.ppermute(passed, ('far', 'core'), mirrored(1, fars))]
    ppermute x1, waiting for transfers between devices: 4.69 us -> 5.86 us  [body(): lax.ppermute(sent, ('far', 'core'), mirrored(0, fars)).astype(jnp.float32)]
where the time goes in v7:
time: 102 us; the launch traced here: 101 us
  starting transfers between devices  45.6 us (45%)
  blocking collectives  28.1 us (28%)
  waiting for transfers between devices  17.1 us (17%)
  Pallas kernels  8.12 us (8%)
  matrix products  1.26 us (1%)
    all_to_all x1, blocking collectives, body(): lax.all_to_all(partial, ('x', 'y'), split_axis=0, concat_axis=0, tiled=True)  28.1 us
    ppermute x1, starting transfers between devices, body(): lax.ppermute(sent, ('far', 'core'), mirrored(0, fars)).astype(jnp.float32)  15.5 us
    all_to_all x1, starting transfers between devices, body(): lax.all_to_all(outgoing, 'expert', split_axis=0, concat_axis=0, tiled=True)  13.1 us
    ppermute x1, starting transfers between devices, body(): passed = lax.ppermute(passed, ('far', 'core'), mirrored(1, fars))  7.64 us
    ppermute x1, starting transfers between devices, body(): met = lax.ppermute(theirs, 'core', SWAP)  7.44 us
    ppermute x1, waiting for transfers between devices, body(): lax.ppermute(sent, ('far', 'core'), mirrored(0, fars)).astype(jnp.float32)  5.86 us
    pallas_call x1, Pallas kernels, hidden_halves(): pl.pallas_call(functools.partial(hidden_kernel, block), in_specs=[pl.Bloc...  5.74 us
    ppermute x1, waiting for transfers between devices, body(): passed = lax.ppermute(passed, ('far', 'core'), mirrored(1, fars))  5.68 us
  transfers between devices with their start and end apart: 5, of which 4 were waited for; matrix products, arithmetic and copies ran while one was open for 1% of the time, Pallas kernels for 6%

profile of v7, /device:TPU:1, one launch (start us, length us, event | category | flops | bytes accessed | tf_op | source)
XLA Modules:
  0.0 100.9 jit_solution(17033448628091115957)
XLA Ops:
  0.0 2.0 %routed.1 = bf16[8,32,256]{2,1,0:T(8,128)(2,1)} custom-call(bf16[128,2048]{1,0:T(8,128)(2,1)} %tokens_from.1, f32[2,128]{1,0:T(2,128)} %bitcast.13, s32[2,128]{1,0:T(2,128)} %bitcast.14), custom_call_target="tpu_custom_call" | custom-call | tf_op jit(solution)/shard_map/routed/pallas_call | solution.py:125
  2.0 13.1 %all-to-all-start = ((bf16[8,32,256]{2,1,0:T(8,128)(2,1)}), bf16[8,32,256]{2,1,0:T(8,128)(2,1)S(1)}, u32[]{:S(2)}, u32[]{:S(2)}) async-start(bf16[8,32,256]{2,1,0:T(8,128)(2,1)} %routed.1), calls=%async_computation | async-start | bytes 262144 | tf_op jit(solution)/shard_map/all_to_all | solution.py:187
  15.1 5.7 %hidden.1 = (bf16[3584,256]{1,0:T(8,128)(2,1)S(1)}, bf16[3584,256]{1,0:T(8,128)(2,1)}) custom-call(s32[1]{0:T(128)} %bitcast.3.core_ref, bf16[256,7168]{1,0:T(8,128)(2,1)} %gate_ref.1, bf16[256,7168]{1,0:T(8,128)(2,1)} %up_ref.1), custom_call_target="tpu_custom_call" | custom-call | flops 14680064 | bytes 11010048 | tf_op jit(solution)/shard_map/hidden/pallas_call | solution.py:65
  20.8 4.5 %all-to-all-done = bf16[8,32,256]{2,1,0:T(8,128)(2,1)S(1)} async-done(((bf16[8,32,256]{2,1,0:T(8,128)(2,1)}), bf16[8,32,256]{2,1,0:T(8,128)(2,1)S(1)}, u32[]{:S(2)}, u32[]{:S(2)}) %all-to-all-start) | async-done | bytes 131104 | tf_op jit(solution)/shard_map/all_to_all | solution.py:187
  25.4 7.4 %collective-permute-start = (bf16[3584,256]{1,0:T(8,128)(2,1)}, bf16[3584,256]{1,0:T(8,128)(2,1)S(1)}, u32[]{:S(2)}, u32[]{:S(2)}) collective-permute-start(bf16[3584,256]{1,0:T(8,128)(2,1)} %get-tuple-element.21), channel_id=1, source_target_pairs={{0,8},{8,0},{1,9},{9,1},{2,10},{10,2},{3,11},{11,3},{4,12},{12,4},... | collective-permute-start | bytes 5505032 | tf_op jit(solution)/shard_map/ppermute | solution.py:190
  32.8 1.9 %collective-permute-start.1 = (bf16[256,256]{1,0:T(8,128)(2,1)S(1)}, bf16[256,256]{1,0:T(8,128)(2,1)S(1)}, u32[]{:S(2)}, u32[]{:S(2)}) collective-permute-start(bf16[256,256]{1,0:T(8,128)(2,1)S(1)} %bitcast.11), channel_id=1, source_target_pairs={{0,8},{8,0},{1,9},{9,1},{2,10},{10,2},{3,11},{11,3},{4,12},{12,4},... | collective-permute-start | bytes 393224 | tf_op jit(solution)/shard_map/ppermute | solution.py:191
  34.7 0.6 fusion.3
  35.4 1.0 %collective-permute-done.1 = bf16[256,256]{1,0:T(8,128)(2,1)S(1)} collective-permute-done((bf16[256,256]{1,0:T(8,128)(2,1)S(1)}, bf16[256,256]{1,0:T(8,128)(2,1)S(1)}, u32[]{:S(2)}, u32[]{:S(2)}) %collective-permute-start.1) | collective-permute-done | bytes 131104 | tf_op jit(solution)/shard_map/ppermute | solution.py:191
  36.4 0.0 collective-permute-done
  36.4 0.6 fusion
  37.0 28.1 %all_to_all.10.terms_ref = bf16[16,224,256]{2,1,0:T(8,128)(2,1)S(1)} all-to-all(bf16[16,224,256]{2,1,0:T(8,128)(2,1)S(1)} %bitcast.10), channel_id=1, replica_groups=mesh['x'=4,'y'=4,'far'=4,'core'=2,'expert'=8] {'x','y'}, dimensions={0} | all-to-all | bytes 3670016 | tf_op jit(solution)/shard_map/all_to_all | solution.py:197
  65.2 0.4 plane_sum.1
  65.6 15.5 %collective-permute-start.2 = (bf16[112,256]{1,0:T(8,128)(2,1)S(1)}, bf16[112,256]{1,0:T(8,128)(2,1)S(1)}, u32[]{:S(2)}, u32[]{:S(2)}) collective-permute-start(bf16[112,256]{1,0:T(8,128)(2,1)S(1)} %get-tuple-element.23), channel_id=1, source_target_pairs={{0,48},{8,24},{16,32},{24,8},{32,16},{40,56},{48,0},{56,40},{1,49}... | collective-permute-start | bytes 172040 | tf_op jit(solution)/shard_map/ppermute | solution.py:199
  81.1 5.9 %collective-permute-done.2 = bf16[112,256]{1,0:T(8,128)(2,1)S(1)} collective-permute-done((bf16[112,256]{1,0:T(8,128)(2,1)S(1)}, bf16[112,256]{1,0:T(8,128)(2,1)S(1)}, u32[]{:S(2)}, u32[]{:S(2)}) %collective-permute-start.2) | collective-permute-done | bytes 57376 | tf_op jit(solution)/shard_map/ppermute | solution.py:199
  87.0 7.6 %collective-permute-start.3 = (bf16[56,256]{1,0:T(8,128)(2,1)S(1)}, bf16[56,256]{1,0:T(8,128)(2,1)S(1)}, u32[]{:S(2)}, u32[]{:S(2)}) collective-permute-start(bf16[56,256]{1,0:T(8,128)(2,1)S(1)} %fusion.1), channel_id=1, source_target_pairs={{0,16},{8,56},{16,0},{24,40},{32,48},{40,24},{48,32},{56,8},{1,17}... | collective-permute-start | bytes 86024 | tf_op jit(solution)/shard_map/ppermute | solution.py:201
  94.6 5.7 %collective-permute-done.3 = bf16[56,256]{1,0:T(8,128)(2,1)S(1)} collective-permute-done((bf16[56,256]{1,0:T(8,128)(2,1)S(1)}, bf16[56,256]{1,0:T(8,128)(2,1)S(1)}, u32[]{:S(2)}, u32[]{:S(2)}) %collective-permute-start.3) | collective-permute-done | bytes 28704 | tf_op jit(solution)/shard_map/ppermute | solution.py:201
  100.3 0.6 fusion.2
  (2 shorter events, 0.0 us)
Async XLA Ops:
  2.0 23.4 %all-to-all-start = ((bf16[8,32,256]{2,1,0:T(8,128)(2,1)}), bf16[8,32,256]{2,1,0:T(8,128)(2,1)S(1)}, u32[]{:S(2)}, u32[]{:S(2)}) async-start(bf16[8,32,256]{2,1,0:T(8,128)(2,1)} %routed.1), calls=%async_computation | async-start | bytes 262144 | tf_op jit(solution)/shard_map/all_to_all | solution.py:187
  25.4 11.0 %collective-permute-start = (bf16[3584,256]{1,0:T(8,128)(2,1)}, bf16[3584,256]{1,0:T(8,128)(2,1)S(1)}, u32[]{:S(2)}, u32[]{:S(2)}) collective-permute-start(bf16[3584,256]{1,0:T(8,128)(2,1)} %get-tuple-element.21), channel_id=1, source_target_pairs={{0,8},{8,0},{1,9},{9,1},{2,10},{10,2},{3,11},{11,3},{4,12},{12,4},... | collective-permute-start | bytes 5505032 | tf_op jit(solution)/shard_map/ppermute | solution.py:190
  32.8 3.6 %collective-permute-start.1 = (bf16[256,256]{1,0:T(8,128)(2,1)S(1)}, bf16[256,256]{1,0:T(8,128)(2,1)S(1)}, u32[]{:S(2)}, u32[]{:S(2)}) collective-permute-start(bf16[256,256]{1,0:T(8,128)(2,1)S(1)} %bitcast.11), channel_id=1, source_target_pairs={{0,8},{8,0},{1,9},{9,1},{2,10},{10,2},{3,11},{11,3},{4,12},{12,4},... | collective-permute-start | bytes 393224 | tf_op jit(solution)/shard_map/ppermute | solution.py:191
  65.6 21.3 %collective-permute-start.2 = (bf16[112,256]{1,0:T(8,128)(2,1)S(1)}, bf16[112,256]{1,0:T(8,128)(2,1)S(1)}, u32[]{:S(2)}, u32[]{:S(2)}) collective-permute-start(bf16[112,256]{1,0:T(8,128)(2,1)S(1)} %get-tuple-element.23), channel_id=1, source_target_pairs={{0,48},{8,24},{16,32},{24,8},{32,16},{40,56},{48,0},{56,40},{1,49}... | collective-permute-start | bytes 172040 | tf_op jit(solution)/shard_map/ppermute | solution.py:199
  87.0 13.3 %collective-permute-start.3 = (bf16[56,256]{1,0:T(8,128)(2,1)S(1)}, bf16[56,256]{1,0:T(8,128)(2,1)S(1)}, u32[]{:S(2)}, u32[]{:S(2)}) collective-permute-start(bf16[56,256]{1,0:T(8,128)(2,1)S(1)} %fusion.1), channel_id=1, source_target_pairs={{0,16},{8,56},{16,0},{24,40},{32,48},{40,24},{48,32},{56,8},{1,17}... | collective-permute-start | bytes 86024 | tf_op jit(solution)/shard_map/ppermute | solution.py:201

commit v8 on v6

--- a/solution.py
+++ b/solution.py
@@ -22,8 +22,9 @@
     ]
 
 
-def hidden_kernel(block, core_ref, gate_ref, up_ref, mine_ref, theirs_ref, gate, up, sems):
+def hidden_kernel(block, side, core_ref, gate_ref, up_ref, mine_ref, theirs_ref, gate, up, sems):
     parts, rows, part = gate.shape
+    rows_of_plane = mine_ref.shape[0] // (side * side)
 
     def copies(index):
         columns = pl.ds(index * part, part)
@@ -45,25 +46,29 @@
         value = value.T.reshape(part // (2 * block), 2, block, rows)
         first = value[:, 0].reshape(part // 2, rows).astype(jnp.bfloat16)
         second = value[:, 1].reshape(part // 2, rows).astype(jnp.bfloat16)
-        where = slice(index * (part // 2), (index + 1) * (part // 2))
-
-        @pl.when(core == 0)
-        def _():
-            mine_ref[where, :] = first
-            theirs_ref[where, :] = second
-
-        @pl.when(core != 0)
-        def _():
-            mine_ref[where, :] = second
-            theirs_ref[where, :] = first
-
-
-def hidden_halves(core, gate_pre, up_pre, block):
+        run = rows_of_plane
+        for piece in range(part // 2 // run):
+            column, row = divmod(index * (part // 2 // run) + piece, side)
+            source = slice(piece * run, (piece + 1) * run)
+            where = slice((row * side + column) * run, (row * side + column + 1) * run)
+
+            @pl.when(core == 0)
+            def _():
+                mine_ref[where, :] = first[source]
+                theirs_ref[where, :] = second[source]
+
+            @pl.when(core != 0)
+            def _():
+                mine_ref[where, :] = second[source]
+                theirs_ref[where, :] = first[source]
+
+
+def hidden_halves(core, gate_pre, up_pre, block, side):
     rows, units = gate_pre.shape
     half = jax.ShapeDtypeStruct((units // 2, rows), jnp.bfloat16)
     buffer = pltpu.VMEM((PARTS, rows, units // PARTS), jnp.bfloat16)
     return pl.pallas_call(
-        functools.partial(hidden_kernel, block),
+        functools.partial(hidden_kernel, block, side),
         in_specs=[
             pl.BlockSpec(memory_space=pltpu.SMEM),
             pl.BlockSpec(memory_space=pl.ANY),
@@ -183,7 +188,7 @@
     outgoing = routed(d_out, router_weight, routes, group_count, capacity)
     place = lax.axis_index(("far", "core"))
     core, place, outgoing = lax.optimization_barrier((core, place, outgoing))
-    mine, theirs = hidden_halves(core, gate_pre, up_pre, block)
+    mine, theirs = hidden_halves(core, gate_pre, up_pre, block, lax.axis_size("x"))
     incoming = lax.all_to_all(outgoing, "expert", split_axis=0, concat_axis=0, tiled=True)
     incoming = incoming.reshape(rows, width)
     theirs, incoming = lax.optimization_barrier((theirs, incoming))
@@ -194,7 +199,7 @@
         met, incoming_met, preferred_element_type=jnp.float32
     )
     partial = partial.astype(jnp.bfloat16).reshape(planes, fars * block, width)
-    partial = lax.all_to_all(partial, ("x", "y"), split_axis=0, concat_axis=0, tiled=True)
+    partial = lax.all_to_all(partial, ("y", "x"), split_axis=0, concat_axis=0, tiled=True)
     own, passed, sent = summed(place, partial, fars)
     sent = lax.ppermute(sent, ("far", "core"), mirrored(0, fars)).astype(jnp.float32)
     passed = (passed + sent[block:]).astype(jnp.bfloat16)

time: 102 us -> 103 us (level)
  no operation moved by 1% of the time
where the time goes in v8:
time: 103 us; the launch traced here: 101 us
  starting transfers between devices  51 us (50%)
  blocking collectives  28.7 us (28%)
  waiting for transfers between devices  11.6 us (11%)
  Pallas kernels  8.13 us (8%)
  matrix products  1.26 us (1%)
    all_to_all x1, blocking collectives, body(): lax.all_to_all(partial, ('y', 'x'), split_axis=0, concat_axis=0, tiled=True)  28.7 us
    ppermute x1, starting transfers between devices, body(): lax.ppermute(sent, ('far', 'core'), mirrored(0, fars)).astype(jnp.float32)  15.2 us
    ppermute x1, starting transfers between devices, body(): passed = lax.ppermute(passed, ('far', 'core'), mirrored(1, fars))  13.4 us
    all_to_all x1, starting transfers between devices, body(): lax.all_to_all(outgoing, 'expert', split_axis=0, concat_axis=0, tiled=True)  13.1 us
    ppermute x1, starting transfers between devices, body(): met = lax.ppermute(theirs, 'core', SWAP)  7.44 us
    pallas_call x1, Pallas kernels, hidden_halves(): pl.pallas_call(functools.partial(hidden_kernel, block, side), in_specs=[p...  5.75 us
    ppermute x1, waiting for transfers between devices, body(): lax.ppermute(sent, ('far', 'core'), mirrored(0, fars)).astype(jnp.float32)  4.69 us
    all_to_all x1, waiting for transfers between devices, body(): lax.all_to_all(outgoing, 'expert', split_axis=0, concat_axis=0, tiled=True)  4.52 us
  transfers between devices with their start and end apart: 5, of which 4 were waited for; matrix products, arithmetic and copies ran while one was open for 1% of the time, Pallas kernels for 6%

profile of v8, /device:TPU:1, one launch (start us, length us, event | category | flops | bytes accessed | tf_op | source)
XLA Modules:
  0.0 101.5 jit_solution(3750563994234970641)
XLA Ops:
  0.0 2.0 %routed.1 = bf16[8,32,256]{2,1,0:T(8,128)(2,1)} custom-call(bf16[128,2048]{1,0:T(8,128)(2,1)} %tokens_from.1, f32[2,128]{1,0:T(2,128)} %bitcast.13, s32[2,128]{1,0:T(2,128)} %bitcast.14), custom_call_target="tpu_custom_call" | custom-call | tf_op jit(solution)/shard_map/routed/pallas_call | solution.py:130
  2.0 13.1 %all-to-all-start = ((bf16[8,32,256]{2,1,0:T(8,128)(2,1)}), bf16[8,32,256]{2,1,0:T(8,128)(2,1)S(1)}, u32[]{:S(2)}, u32[]{:S(2)}) async-start(bf16[8,32,256]{2,1,0:T(8,128)(2,1)} %routed.1), calls=%async_computation | async-start | bytes 262144 | tf_op jit(solution)/shard_map/all_to_all | solution.py:192
  15.1 5.8 %hidden.1 = (bf16[3584,256]{1,0:T(8,128)(2,1)S(1)}, bf16[3584,256]{1,0:T(8,128)(2,1)}) custom-call(s32[1]{0:T(128)} %bitcast.3.core_ref, bf16[256,7168]{1,0:T(8,128)(2,1)} %gate_ref.1, bf16[256,7168]{1,0:T(8,128)(2,1)} %up_ref.1), custom_call_target="tpu_custom_call" | custom-call | flops 14680064 | bytes 11010048 | tf_op jit(solution)/shard_map/hidden/pallas_call | solution.py:70
  20.8 4.5 %all-to-all-done = bf16[8,32,256]{2,1,0:T(8,128)(2,1)S(1)} async-done(((bf16[8,32,256]{2,1,0:T(8,128)(2,1)}), bf16[8,32,256]{2,1,0:T(8,128)(2,1)S(1)}, u32[]{:S(2)}, u32[]{:S(2)}) %all-to-all-start) | async-done | bytes 131104 | tf_op jit(solution)/shard_map/all_to_all | solution.py:192
  25.4 7.4 %collective-permute-start = (bf16[3584,256]{1,0:T(8,128)(2,1)}, bf16[3584,256]{1,0:T(8,128)(2,1)S(1)}, u32[]{:S(2)}, u32[]{:S(2)}) collective-permute-start(bf16[3584,256]{1,0:T(8,128)(2,1)} %get-tuple-element.21), channel_id=1, source_target_pairs={{0,8},{8,0},{1,9},{9,1},{2,10},{10,2},{3,11},{11,3},{4,12},{12,4},... | collective-permute-start | bytes 5505032 | tf_op jit(solution)/shard_map/ppermute | solution.py:195
  32.8 1.9 %collective-permute-start.1 = (bf16[256,256]{1,0:T(8,128)(2,1)S(1)}, bf16[256,256]{1,0:T(8,128)(2,1)S(1)}, u32[]{:S(2)}, u32[]{:S(2)}) collective-permute-start(bf16[256,256]{1,0:T(8,128)(2,1)S(1)} %bitcast.11), channel_id=1, source_target_pairs={{0,8},{8,0},{1,9},{9,1},{2,10},{10,2},{3,11},{11,3},{4,12},{12,4},... | collective-permute-start | bytes 393224 | tf_op jit(solution)/shard_map/ppermute | solution.py:196
  34.7 0.6 fusion.3
  35.4 1.0 %collective-permute-done.1 = bf16[256,256]{1,0:T(8,128)(2,1)S(1)} collective-permute-done((bf16[256,256]{1,0:T(8,128)(2,1)S(1)}, bf16[256,256]{1,0:T(8,128)(2,1)S(1)}, u32[]{:S(2)}, u32[]{:S(2)}) %collective-permute-start.1) | collective-permute-done | bytes 131104 | tf_op jit(solution)/shard_map/ppermute | solution.py:196
  36.4 0.0 collective-permute-done
  36.4 0.6 fusion
  37.0 28.7 %all_to_all.10.terms_ref = bf16[16,224,256]{2,1,0:T(8,128)(2,1)S(1)} all-to-all(bf16[16,224,256]{2,1,0:T(8,128)(2,1)S(1)} %bitcast.10), channel_id=1, replica_groups=mesh['x'=4,'y'=4,'far'=4,'core'=2,'expert'=8] {'y','x'}, dimensions={0} | all-to-all | bytes 3670016 | tf_op jit(solution)/shard_map/all_to_all | solution.py:202
  65.7 0.4 plane_sum.1
  66.1 15.2 %collective-permute-start.2 = (bf16[112,256]{1,0:T(8,128)(2,1)S(1)}, bf16[112,256]{1,0:T(8,128)(2,1)S(1)}, u32[]{:S(2)}, u32[]{:S(2)}) collective-permute-start(bf16[112,256]{1,0:T(8,128)(2,1)S(1)} %get-tuple-element.23), channel_id=1, source_target_pairs={{0,16},{8,56},{16,0},{24,40},{32,48},{40,24},{48,32},{56,8},{1,17}... | collective-permute-start | bytes 172040 | tf_op jit(solution)/shard_map/ppermute | solution.py:204
  81.4 4.7 %collective-permute-done.2 = bf16[112,256]{1,0:T(8,128)(2,1)S(1)} collective-permute-done((bf16[112,256]{1,0:T(8,128)(2,1)S(1)}, bf16[112,256]{1,0:T(8,128)(2,1)S(1)}, u32[]{:S(2)}, u32[]{:S(2)}) %collective-permute-start.2) | collective-permute-done | bytes 57376 | tf_op jit(solution)/shard_map/ppermute | solution.py:204
  86.1 13.4 %collective-permute-start.3 = (bf16[56,256]{1,0:T(8,128)(2,1)S(1)}, bf16[56,256]{1,0:T(8,128)(2,1)S(1)}, u32[]{:S(2)}, u32[]{:S(2)}) collective-permute-start(bf16[56,256]{1,0:T(8,128)(2,1)S(1)} %fusion.1), channel_id=1, source_target_pairs={{0,48},{8,24},{16,32},{24,8},{32,16},{40,56},{48,0},{56,40},{1,49}... | collective-permute-start | bytes 86024 | tf_op jit(solution)/shard_map/ppermute | solution.py:206
  99.5 1.4 %collective-permute-done.3 = bf16[56,256]{1,0:T(8,128)(2,1)S(1)} collective-permute-done((bf16[56,256]{1,0:T(8,128)(2,1)S(1)}, bf16[56,256]{1,0:T(8,128)(2,1)S(1)}, u32[]{:S(2)}, u32[]{:S(2)}) %collective-permute-start.3) | collective-permute-done | bytes 28704 | tf_op jit(solution)/shard_map/ppermute | solution.py:206
  100.8 0.6 fusion.2
  (2 shorter events, 0.0 us)
Async XLA Ops:
  2.0 23.4 %all-to-all-start = ((bf16[8,32,256]{2,1,0:T(8,128)(2,1)}), bf16[8,32,256]{2,1,0:T(8,128)(2,1)S(1)}, u32[]{:S(2)}, u32[]{:S(2)}) async-start(bf16[8,32,256]{2,1,0:T(8,128)(2,1)} %routed.1), calls=%async_computation | async-start | bytes 262144 | tf_op jit(solution)/shard_map/all_to_all | solution.py:192
  25.4 11.0 %collective-permute-start = (bf16[3584,256]{1,0:T(8,128)(2,1)}, bf16[3584,256]{1,0:T(8,128)(2,1)S(1)}, u32[]{:S(2)}, u32[]{:S(2)}) collective-permute-start(bf16[3584,256]{1,0:T(8,128)(2,1)} %get-tuple-element.21), channel_id=1, source_target_pairs={{0,8},{8,0},{1,9},{9,1},{2,10},{10,2},{3,11},{11,3},{4,12},{12,4},... | collective-permute-start | bytes 5505032 | tf_op jit(solution)/shard_map/ppermute | solution.py:195
  32.8 3.6 %collective-permute-start.1 = (bf16[256,256]{1,0:T(8,128)(2,1)S(1)}, bf16[256,256]{1,0:T(8,128)(2,1)S(1)}, u32[]{:S(2)}, u32[]{:S(2)}) collective-permute-start(bf16[256,256]{1,0:T(8,128)(2,1)S(1)} %bitcast.11), channel_id=1, source_target_pairs={{0,8},{8,0},{1,9},{9,1},{2,10},{10,2},{3,11},{11,3},{4,12},{12,4},... | collective-permute-start | bytes 393224 | tf_op jit(solution)/shard_map/ppermute | solution.py:196
  66.1 19.9 %collective-permute-start.2 = (bf16[112,256]{1,0:T(8,128)(2,1)S(1)}, bf16[112,256]{1,0:T(8,128)(2,1)S(1)}, u32[]{:S(2)}, u32[]{:S(2)}) collective-permute-start(bf16[112,256]{1,0:T(8,128)(2,1)S(1)} %get-tuple-element.23), channel_id=1, source_target_pairs={{0,16},{8,56},{16,0},{24,40},{32,48},{40,24},{48,32},{56,8},{1,17}... | collective-permute-start | bytes 172040 | tf_op jit(solution)/shard_map/ppermute | solution.py:204
  86.1 14.7 %collective-permute-start.3 = (bf16[56,256]{1,0:T(8,128)(2,1)S(1)}, bf16[56,256]{1,0:T(8,128)(2,1)S(1)}, u32[]{:S(2)}, u32[]{:S(2)}) collective-permute-start(bf16[56,256]{1,0:T(8,128)(2,1)S(1)} %fusion.1), channel_id=1, source_target_pairs={{0,48},{8,24},{16,32},{24,8},{32,16},{40,56},{48,0},{56,40},{1,49}... | collective-permute-start | bytes 86024 | tf_op jit(solution)/shard_map/ppermute | solution.py:206
